TPU v7x, 32 devices: a whole 2x2x4 slice. The times are simulated.
32 devices in a mesh: subj: 4 (over y, x), gz: 8 (over z, core).
Axes of the slice: x: 2, y: 2, z: 4, core: 2. Of those that a mesh axis runs over, the one named last changes fastest.
Arguments:
- warped: float32 [4, 256, 64, 256], P('subj', 'gz'), may hold values from -12 to 12
Outputs:
- force: float32 [4, 3, 256, 64, 256], P('subj', None, 'gz')
- template: float32 [256, 64, 256], P('gz')
- loss: float32 [4], P('subj')
All inputs are finite; a program needn't handle non-finite values.
Results may differ from a plain program's by a relative error of at most 0.0001.
Values sent between devices are 32-bit elements; how exact they have to be, the bound alone decides.
A program may use at most 128 MiB of HBM per device.

v0:
```python
import math

import jax
import jax.numpy as jnp
from jax import lax
from jax.sharding import PartitionSpec as P

BOX_R = 4
GAUSS_R = 3


epsilon = 1e-05


def padded_2(array, sides, width):
    for axis, dim in sides:
        size, length = (lax.axis_size(axis), array.shape[dim])
        up = [(i, (i + 1) % size) for i in range(size - 1)]
        down = [(j, i) for i, j in up]
        last = lax.slice_in_dim(array, length - width, length, axis=dim)
        first = lax.slice_in_dim(array, 0, width, axis=dim)
        before = lax.ppermute(last, axis, up)
        after = lax.ppermute(first, axis, down)
        array = jnp.concatenate([before, array, after], axis=dim)
    return array


def shifted_sum(padded, along, planes_out, window_span):
    running = lax.slice_in_dim(padded, 0, planes_out, axis=along)
    for offset in range(1, window_span):
        running = running + lax.slice_in_dim(padded, offset, offset + planes_out, axis=along)
    return running


def window_mean(volume):
    window_span = 2 * BOX_R + 1
    planes_out = volume.shape[0] - 2 * BOX_R
    running = shifted_sum(volume, 0, planes_out, window_span)
    running = shifted_sum(
        jnp.pad(running, ((0, 0), (BOX_R, BOX_R), (0, 0))), 1, volume.shape[1], window_span
    )
    running = shifted_sum(
        jnp.pad(running, ((0, 0), (0, 0), (BOX_R, BOX_R))), 2, volume.shape[2], window_span
    )
    return running / float(window_span**3)


def local_force(moving, target):
    planes_out = moving.shape[0] - 2 * BOX_R
    mean_moving = window_mean(moving)
    mean_target = window_mean(target)
    var_moving = window_mean(moving * moving) - mean_moving * mean_moving
    var_target = window_mean(target * target) - mean_target * mean_target
    cross_cov = window_mean(moving * target) - mean_moving * mean_target
    moving_core = moving[BOX_R : BOX_R + planes_out]
    target_core = target[BOX_R : BOX_R + planes_out]
    denominator = var_moving * var_target + epsilon
    similarity = cross_cov * cross_cov / denominator
    factor = (
        2.0
        * cross_cov
        / denominator
        * (
            target_core
            - mean_target
            - cross_cov / (var_moving + epsilon) * (moving_core - mean_moving)
        )
    )
    slope_depth = 0.5 * (
        moving[BOX_R + 1 : BOX_R + 1 + planes_out] - moving[BOX_R - 1 : BOX_R - 1 + planes_out]
    )
    padded_rows = jnp.pad(moving_core, ((0, 0), (1, 1), (0, 0)))
    slope_rows = 0.5 * (padded_rows[:, 2:] - padded_rows[:, :-2])
    padded_cols = jnp.pad(moving_core, ((0, 0), (0, 0), (1, 1)))
    slope_cols = 0.5 * (padded_cols[:, :, 2:] - padded_cols[:, :, :-2])
    forces = jnp.stack([factor * slope_depth, factor * slope_rows, factor * slope_cols])
    return (forces, similarity)


def blur_weights():
    bumps = [math.exp(-(offset * offset) / 8.0) for offset in range(-GAUSS_R, GAUSS_R + 1)]
    whole = sum(bumps)
    return [bump / whole for bump in bumps]


def weighted_sum(padded, along, planes_out, weights):
    running = weights[0] * lax.slice_in_dim(padded, 0, planes_out, axis=along)
    for offset in range(1, len(weights)):
        running = running + weights[offset] * lax.slice_in_dim(
            padded, offset, offset + planes_out, axis=along
        )
    return running


def gaussian_blur(padded):
    weights = blur_weights()
    planes_out = padded.shape[1] - 2 * GAUSS_R
    smoothed = weighted_sum(padded, 1, planes_out, weights)
    smoothed = weighted_sum(
        jnp.pad(smoothed, ((0, 0), (0, 0), (GAUSS_R, GAUSS_R), (0, 0))), 2, padded.shape[2], weights
    )
    smoothed = weighted_sum(
        jnp.pad(smoothed, ((0, 0), (0, 0), (0, 0), (GAUSS_R, GAUSS_R))), 3, padded.shape[3], weights
    )
    return smoothed


def on_device(warped):
    moving = warped[0]
    planes = moving.shape[0]
    members = lax.axis_size("subj")
    halo_depth = BOX_R
    moving_wide = padded_2(moving, (("gz", 0),), halo_depth)
    target_wide = lax.psum(moving_wide, "subj") / members
    template = target_wide[halo_depth : halo_depth + planes]
    forces, similarity = local_force(moving_wide, target_wide)
    padded = padded_2(forces, (("gz", 1),), GAUSS_R)
    smoothed = gaussian_blur(padded)
    cells = float(lax.axis_size("gz") * planes * moving.shape[1] * moving.shape[2])
    loss = -lax.psum(jnp.sum(similarity), "gz") / cells
    return (smoothed[None], template, jnp.reshape(loss, (1,)))


def solution(mesh):
    placed = (P("subj", "gz", None, None),)
    return jax.shard_map(
        on_device,
        mesh=mesh,
        in_specs=placed,
        out_specs=(P("subj", None, "gz", None, None), P("gz", None, None), P("subj")),
        check_vma=False,
    )
```

profile of v0, /device:TPU:0, one launch (start us, length us, event | category | flops | bytes accessed | tf_op | source)
XLA Modules:
  0.0 282.7 jit_solution(15680484089555953680)
XLA Ops:
  7.2 0.0 all-reduce.16.cloned.1.call-start
  7.2 1.1 slice_bitcast_fusion
  8.3 1.3 collective-permute-start.1
  9.6 3.0 %collective-permute-start = (f32[4,64,256]{2,1,0:T(8,128)S(1)}, f32[4,64,256]{2,1,0:T(8,128)S(1)}, u32[]{:S(2)}, u32[]{:S(2)}) collective-permute-start(f32[4,64,256]{2,1,0:T(8,128)S(1)} %get-tuple-element.24), channel_id=1, source_target_pairs={{0,1},{1,2},{2,3},{3,4},{4,5},{5,6},{6,7},{8,9},{9,10},{10,11},{11... | collective-permute-start | bytes 786440 | tf_op jit(solution)/shard_map/ppermute | solution.py:22
  12.6 0.0 collective-permute-done.1
  12.7 1.1 collective-permute-done
  13.8 0.0 copy-start.10
  13.8 3.5 %pad_maximum_fusion.2 = f32[40,64,256]{2,1,0:T(8,128)} fusion(f32[4,64,256]{2,1,0:T(8,128)S(1)} %collective-permute-done.1, f32[32,64,256]{2,1,0:T(8,128)} %bitcast.16, f32[4,64,256]{2,1,0:T(8,128)S(1)} %collective-permute-done), kind=kLoop, calls=%fused_computation.100 | loop fusion | flops 1310720 | bytes 5242880 | tf_op jit(solution)/shard_map/concatenate | solution.py:24
  17.3 0.0 copy-start
  17.3 0.0 all-reduce.16.cloned.1.call-update
  17.3 0.0 copy-done.10
  17.3 1.6 copy-done
  18.8 2.4 fusion.73
  21.3 2.7 fusion.46
  24.0 78.7 %all-reduce.16.cloned.1.call-done = f32[40,64,256]{2,1,0:T(8,128)} async-done(((f32[40,64,256]{2,1,0:T(8,128)}), f32[40,64,256]{2,1,0:T(8,128)}) %all-reduce.16.cloned.1.call-update) | async-done | bytes 2621456 | tf_op jit(solution)/shard_map/psum | solution.py:114
  102.7 3.4 %broadcast_multiply_fusion = (f32[40,64,256]{2,1,0:T(8,128)S(1)}, f32[40,64,256]{2,1,0:T(8,128)S(1)}, f32[40,64,256]{2,1,0:T(8,128)S(1)}, f32[40,64,256]{2,1,0:T(8,128)S(1)}) fusion(f32[40,64,256]{2,1,0:T(8,128)} %all-reduce.16.cloned.1.call-done, f32[4,64,256]{2,1,0:T(8,128)S(1)} %collective-permute-done.1, f32[32,64,256]{2,1,0:T(8,128)S(1)} %bitcast.18, ...), kind=kLoop, calls=%fused_computation.302 | loop fusion | flops 3932160 | bytes 15728640 | tf_op jit(solution)/shard_map/div | solution.py:114
  106.1 5.8 %slice_add_fusion.16 = (f32[32,64,256]{2,1,0:T(8,128)}, f32[32,64,256]{2,1,0:T(8,128)}, f32[32,64,256]{2,1,0:T(8,128)}) fusion(f32[40,64,256]{2,1,0:T(8,128)S(1)} %get-tuple-element.19, f32[40,64,256]{2,1,0:T(8,128)S(1)} %get-tuple-element.20), kind=kLoop, calls=%fused_computation.277 | loop fusion | flops 8388608 | bytes 44040192 | tf_op jit(solution)/shard_map/add | solution.py:31
  111.9 0.0 copy-start.9
  111.9 9.8 %fusion.54 = f32[32,64,256]{2,1,0:T(8,128)S(1)} fusion(f32[32,64,256]{2,1,0:T(8,128)} %get-tuple-element.11), kind=kLoop, calls=%fused_computation.172 | loop fusion | flops 4194304 | bytes 4194304 | tf_op jit(solution)/shard_map/add | solution.py:31
  121.7 0.0 copy-done.9
  121.7 2.7 fusion.38
  124.4 5.6 %slice_add_fusion = (f32[32,64,256]{2,1,0:T(8,128)S(1)}, f32[32,64,256]{2,1,0:T(8,128)}) fusion(f32[40,64,256]{2,1,0:T(8,128)S(1)} %get-tuple-element.22, f32[40,64,256]{2,1,0:T(8,128)S(1)} %get-tuple-element.21), kind=kLoop, calls=%fused_computation.261 | loop fusion | flops 8388608 | bytes 41943040 | tf_op jit(solution)/shard_map/add | solution.py:31
  130.1 0.0 copy-start.8
  130.1 2.7 fusion.70
  132.8 0.0 copy-done.8
  132.8 0.0 copy-start.7
  132.8 2.7 fusion.62
  135.5 0.0 copy-done.7
  135.5 33.1 %fusion.148 = (f32[]{:T(128)}, f32[32,64,256]{2,1,0:T(8,128)}, f32[32,64,256]{2,1,0:T(8,128)}, f32[32,64,256]{2,1,0:T(8,128)}, f32[32,64,256]{2,1,0:T(8,128)}, /*index=5*/f32[32,64,256]{2,1,0:T(8,128)}) fusion(f32[32,64,256]{2,1,0:T(8,128)} %fusion.70, f32[32,64,256]{2,1,0:T(8,128)} %fusion.62, f32[32,64,256]{2,1,0:T(8,128)} %fusion.38, ...), kind=kLoop, calls=%fused_computation.301 | loop fusion | flops 29360128 | bytes 20971524 | tf_op jit(solution)/shard_map/reduce_sum | solution.py:120
  168.6 5.8 %fusion.147 = (f32[1,32,64,256]{3,2,1,0:T(8,128)S(1)}, f32[32,64,256]{2,1,0:T(8,128)S(1)}) fusion(f32[32,64,256]{2,1,0:T(8,128)S(1)} %bitcast.19, f32[4,64,256]{2,1,0:T(8,128)} %copy-done.10, f32[4,64,256]{2,1,0:T(8,128)S(1)} %collective-permute-done.1, f32[32,64,256]{2,1,0:T(8,128)} %get-tuple-element.8, f32[1,32,64,256]{3,2,1,0:T(8,128)S(1)} %copy-done, ...), kind=kLoop, calls=%fused_computation.290 | loop fusion | flops 7340032 | bytes 21495808 | tf_op jit(solution)/shard_map/stack | solution.py:76
  174.4 0.0 copy-start.5
  174.4 1.3 fusion.88
  175.7 0.0 copy-start.1
  175.7 0.0 copy-start.3
  175.7 0.0 copy-done.5
  175.7 0.5 pad_maximum_fusion.1
  176.2 0.8 copy-done.1
  177.0 0.7 copy-done.3
  177.7 1.2 fusion.157
  178.8 2.6 collective-permute-start.2
  181.4 1.3 collective-permute-start.3
  182.7 18.7 %psum.15 = f32[]{:T(128)} all-reduce(f32[]{:T(128)} %get-tuple-element.3), channel_id=1, replica_groups=mesh['subj'=4,'gz'=8] {'gz'}, use_global_device_ids=true, to_apply=%region_2.3 | all-reduce | flops 1 | bytes 8 | tf_op jit(solution)/shard_map/psum | solution.py:120
  202.1 0.0 copy-start.2
  202.1 0.0 copy-start.4
  202.2 0.0 copy-start.6
  202.2 0.0 collective-permute-done.2
  202.2 0.0 collective-permute-done.3
  202.2 10.5 %maximum_maximum_fusion = (f32[3,35,64,256]{3,2,1,0:T(8,128)}, f32[3,35,64,256]{3,2,1,0:T(8,128)}) fusion(f32[1,32,64,256]{3,2,1,0:T(8,128)} %copy-done.3, f32[1,32,64,256]{3,2,1,0:T(8,128)} %copy-done.1, f32[1,32,64,256]{3,2,1,0:T(8,128)} %copy-done.5, f32[3,3,64,256]{3,2,1,0:T(8,128)} %collective-permute-done.2, f32[3,3,64,256]{3,2,1,0:T(8,128)} %collective-permute-done.3), kind=kLoop, calls=%fused_computation.12 | loop fusion | flops 10321920 | bytes 21233664 | tf_op jit(solution)/shard_map/concatenate | solution.py:24
  212.7 0.0 copy-done.2
  212.7 0.0 copy-done.4
  212.7 0.0 copy-done.6
  212.7 17.4 %fusion.25 = f32[3,32,64,256]{3,2,1,0:T(8,128)} fusion(f32[3,35,64,256]{3,2,1,0:T(8,128)} %get-tuple-element.14, f32[3,35,64,256]{3,2,1,0:T(8,128)} %get-tuple-element.13, f32[1,32,64,256]{3,2,1,0:T(8,128)S(1)} %copy-done.4, f32[1,32,64,256]{3,2,1,0:T(8,128)S(1)} %copy-done.2, f32[1,32,64,256]{3,2,1,0:T(8,128)S(1)} %copy-done.6), kind=kLoop, calls=%fused_computation.40 | loop fusion | flops 23592960 | bytes 50331648 | tf_op jit(solution)/shard_map/add | solution.py:89
  230.1 19.3 %fusion.6 = f32[3,32,64,256]{3,2,1,0:T(8,128)} fusion(f32[3,32,64,256]{3,2,1,0:T(8,128)} %fusion.25), kind=kLoop, calls=%fused_computation.20 | loop fusion | flops 20447232 | bytes 12582912 | tf_op jit(solution)/shard_map/add | solution.py:89
  249.4 25.3 %fusion.19 = f32[1,3,32,64,256]{4,3,2,1,0:T(8,128)} fusion(f32[3,32,64,256]{3,2,1,0:T(8,128)} %fusion.6), kind=kLoop, calls=%fused_computation.33 | loop fusion | flops 20447232 | bytes 12582912 | tf_op jit(solution)/shard_map/broadcast_in_dim | solution.py:121
Async XLA Ops:
  7.2 95.5 %all-reduce.16.cloned.1.call-start = ((), (), s32[]{:S(2)}) async-start(), calls=%async_computation | async-start | bytes 5242880 | tf_op jit(solution)/shard_map/psum | solution.py:114
  8.3 4.4 %collective-permute-start.1 = (f32[4,64,256]{2,1,0:T(8,128)S(1)}, f32[4,64,256]{2,1,0:T(8,128)S(1)}, u32[]{:S(2)}, u32[]{:S(2)}) collective-permute-start(f32[4,64,256]{2,1,0:T(8,128)S(1)} %get-tuple-element.23), channel_id=1, source_target_pairs={{1,0},{2,1},{3,2},{4,3},{5,4},{6,5},{7,6},{9,8},{10,9},{11,10},{12... | collective-permute-start | bytes 786440 | tf_op jit(solution)/shard_map/ppermute | solution.py:23
  9.6 4.2 %collective-permute-start = (f32[4,64,256]{2,1,0:T(8,128)S(1)}, f32[4,64,256]{2,1,0:T(8,128)S(1)}, u32[]{:S(2)}, u32[]{:S(2)}) collective-permute-start(f32[4,64,256]{2,1,0:T(8,128)S(1)} %get-tuple-element.24), channel_id=1, source_target_pairs={{0,1},{1,2},{2,3},{3,4},{4,5},{5,6},{6,7},{8,9},{9,10},{10,11},{11... | collective-permute-start | bytes 786440 | tf_op jit(solution)/shard_map/ppermute | solution.py:22
  13.8 3.5 %copy-start.10 = (f32[4,64,256]{2,1,0:T(8,128)}, f32[4,64,256]{2,1,0:T(8,128)S(1)}, u32[]{:S(2)}) copy-start(f32[4,64,256]{2,1,0:T(8,128)S(1)} %collective-permute-done) | copy-start | bytes 786436
  17.3 1.6 copy-start
  111.9 9.8 %copy-start.9 = (f32[32,64,256]{2,1,0:T(8,128)S(1)}, f32[32,64,256]{2,1,0:T(8,128)}, u32[]{:S(2)}) copy-start(f32[32,64,256]{2,1,0:T(8,128)} %get-tuple-element.27) | copy-start | bytes 6291460
  130.1 2.7 copy-start.8
  132.8 2.7 copy-start.7
  174.4 1.3 copy-start.5
  175.7 1.3 copy-start.1
  175.7 2.0 copy-start.3
  178.8 23.3 %collective-permute-start.2 = (f32[3,3,64,256]{3,2,1,0:T(8,128)}, f32[3,3,64,256]{3,2,1,0:T(8,128)}, u32[]{:S(2)}, u32[]{:S(2)}) collective-permute-start(f32[3,3,64,256]{3,2,1,0:T(8,128)} %get-tuple-element.15), channel_id=1, source_target_pairs={{0,1},{1,2},{2,3},{3,4},{4,5},{5,6},{6,7},{8,9},{9,10},{10,11},{11... | collective-permute-start | bytes 1769480 | tf_op jit(solution)/shard_map/ppermute | solution.py:22
  181.4 20.7 %collective-permute-start.3 = (f32[3,3,64,256]{3,2,1,0:T(8,128)}, f32[3,3,64,256]{3,2,1,0:T(8,128)}, u32[]{:S(2)}, u32[]{:S(2)}) collective-permute-start(f32[3,3,64,256]{3,2,1,0:T(8,128)} %get-tuple-element.16), channel_id=1, source_target_pairs={{1,0},{2,1},{3,2},{4,3},{5,4},{6,5},{7,6},{9,8},{10,9},{11,10},{12... | collective-permute-start | bytes 1769480 | tf_op jit(solution)/shard_map/ppermute | solution.py:23
  202.1 10.6 %copy-start.2 = (f32[1,32,64,256]{3,2,1,0:T(8,128)S(1)}, f32[1,32,64,256]{3,2,1,0:T(8,128)}, u32[]{:S(2)}) copy-start(f32[1,32,64,256]{3,2,1,0:T(8,128)} %copy-done.1) | copy-start | bytes 6291460
  202.1 10.5 %copy-start.4 = (f32[1,32,64,256]{3,2,1,0:T(8,128)S(1)}, f32[1,32,64,256]{3,2,1,0:T(8,128)}, u32[]{:S(2)}) copy-start(f32[1,32,64,256]{3,2,1,0:T(8,128)} %copy-done.3) | copy-start | bytes 6291460
  202.2 10.5 %copy-start.6 = (f32[1,32,64,256]{3,2,1,0:T(8,128)S(1)}, f32[1,32,64,256]{3,2,1,0:T(8,128)}, u32[]{:S(2)}) copy-start(f32[1,32,64,256]{3,2,1,0:T(8,128)} %copy-done.5) | copy-start | bytes 6291460
Sparse Core Ops, SparseCore 0:
  17.4 85.2 all-reduce.15
where the time goes:
time: 283 us
  other arithmetic  154 us (54%)
  waiting for transfers between devices  79.9 us (28%)
  blocking collectives  18.7 us (7%)
  between operations  16 us (6%)
  starting transfers between devices  8.25 us (3%)
  local copies, waits for them, and re-layouts  5.36 us (2%)
    psum x1, waiting for transfers between devices, on_device(): target_wide = lax.psum(moving_wide, 'subj') / members  78.7 us
    add x2, other arithmetic, weighted_sum(): running + weights[offset] * lax.slice_in_dim(padded, offset, offset + pla...  36.7 us
    add x8, other arithmetic, shifted_sum(): running + lax.slice_in_dim(padded, offset, offset + planes_out, axis=along)  34.5 us
    reduce_sum x1, other arithmetic, on_device(): loss = -lax.psum(jnp.sum(similarity), 'gz') / cells  33.1 us
    broadcast_in_dim x1, other arithmetic, on_device(): return (smoothed[None], template, jnp.reshape(loss, (1,)))  25.3 us
    psum x1, blocking collectives, on_device(): loss = -lax.psum(jnp.sum(similarity), 'gz') / cells  18.7 us
    concatenate x2, other arithmetic, padded_2(): array = jnp.concatenate([before, array, after], axis=dim)  14 us
    another operation x3, other arithmetic, local_force(): jnp.stack([factor * slope_depth, factor * slope_rows, factor * slope_cols])  7.55 us
  transfers between devices with their start and end apart: 5, of which 2 were waited for; matrix products, arithmetic and copies ran while one was open for 2% of the time, Pallas kernels for 0%

commit v1 on v0

v1 whole, which is shorter than its diff:
```python
import functools
import math

import jax
import jax.numpy as jnp
import ml_dtypes
import numpy as np
from jax import lax
from jax.experimental import pallas as pl
from jax.experimental.pallas import tpu as pltpu
from jax.sharding import PartitionSpec as P

BOX_R = 4
GAUSS_R = 3
HALO = BOX_R + GAUSS_R
EPS = 1e-05
BLOCK = 8
GROUP = 4
STRIP = 16
F32 = jnp.float32
BF16 = jnp.bfloat16


def bands(rows, cols):
    bumps = np.array([math.exp(-(k * k) / 8.0) for k in range(-GAUSS_R, GAUSS_R + 1)])
    bumps = bumps / bumps.sum()

    def band(n, weights, radius):
        out = np.zeros((n, n), np.float32)
        for k in range(-radius, radius + 1):
            out += np.diag(np.full(n - abs(k), weights[k + radius], np.float32), k)
        return out

    def high_low(m):
        high = m.astype(ml_dtypes.bfloat16)
        low = (m - high.astype(np.float32)).astype(ml_dtypes.bfloat16)
        return high, low

    ones = np.ones(2 * BOX_R + 1)
    eye = np.eye(GROUP, dtype=np.float32)
    box_y = np.kron(eye, band(rows, ones, BOX_R)).astype(ml_dtypes.bfloat16)
    box_x = band(cols, ones, BOX_R).astype(ml_dtypes.bfloat16)
    gy_high, gy_low = high_low(np.kron(eye, band(rows, bumps, GAUSS_R)))
    gx_high, gx_low = high_low(band(cols, bumps, GAUSS_R))
    return (
        np.concatenate([box_y] * 3, axis=1),
        np.concatenate([box_x] * 3, axis=0),
        np.concatenate([gy_high, gy_high, gy_low], axis=1),
        np.concatenate([gx_high, gx_high, gx_low], axis=0),
        [float(b) for b in bumps[GAUSS_R:]],
    )


def split3(v):
    a = v.astype(BF16)
    r = v - a.astype(F32)
    b = r.astype(BF16)
    c = (r - b.astype(F32)).astype(BF16)
    return a, b, c


def split2(v):
    a = v.astype(BF16)
    return a, (v - a.astype(F32)).astype(BF16)


def windows(planes):
    n = BLOCK
    span = 2 * BOX_R + 1
    head = [None] * (n + 1)
    acc = planes[n - 1]
    head[n - 1] = acc
    for i in range(n - 2, -1, -1):
        acc = acc + planes[i]
        head[i] = acc
    out = []
    tail = None
    for i in range(n):
        tail = planes[n + i] if tail is None else tail + planes[n + i]
        out.append(head[i] + tail)
    assert span == n + 1
    return out


def cov_block(b, z_first, depth, planes, iw, jw, r_ref, xy, t_ref, loss, by, bx):
    rows, cols = iw.shape[1], iw.shape[2]
    base = b * BLOCK
    grows = GROUP * rows

    def strip(s, _):
        row = pl.multiple_of(s * STRIP, STRIP)
        for lane in range(0, cols, 128):
            span = BLOCK + 2 * BOX_R
            iv = [iw[base + k, pl.ds(row, STRIP), pl.ds(lane, 128)] for k in range(span)]
            jv = [jw[base + k, pl.ds(row, STRIP), pl.ds(lane, 128)] for k in range(span)]
            for v in range(5):
                if v == 0:
                    vol = iv
                elif v == 1:
                    vol = jv
                elif v == 2:
                    vol = [a * a for a in iv]
                elif v == 3:
                    vol = [a * a for a in jv]
                else:
                    vol = [a * c for a, c in zip(iv, jv)]
                for w, total in enumerate(windows(vol)):
                    g, u = w // GROUP, w % GROUP
                    for k, piece in enumerate(split3(total)):
                        at = k * grows + u * rows
                        xy[v, g, pl.ds(at + row, STRIP), pl.ds(lane, 128)] = piece
        return 0

    lax.fori_loop(0, rows // STRIP, strip, 0)

    scale = 1.0 / float((2 * BOX_R + 1) ** 3)

    def group(g, _):
        for v in range(5):
            ys = jnp.dot(by[...], xy[v, g], preferred_element_type=F32)
            xs = jnp.concatenate(split3(ys), axis=1)
            t_ref[v] = jnp.dot(xs, bx[...], preferred_element_type=F32)

        def plane(u, _):
            at = pl.multiple_of(u * rows, rows)
            c = base + g * GROUP + u
            m = [t_ref[v, pl.ds(at, rows), :] * scale for v in range(5)]
            mi, mj = m[0], m[1]
            var_i = m[2] - mi * mi
            var_j = m[3] - mj * mj
            cc = m[4] - mi * mj
            moving = iw[c + BOX_R]
            target = jw[c + BOX_R]
            q = cc / (var_i * var_j + EPS)
            z = z_first - GAUSS_R + c
            owned = jnp.logical_and(c >= GAUSS_R, c < GAUSS_R + planes)
            sim = jnp.where(owned, cc * q, 0.0)
            loss[...] += sim
            factor = q * ((target - mj) - cc / (var_i + EPS) * (moving - mi))
            inside = jnp.logical_and(z >= 0, z < depth)
            factor = jnp.where(inside, factor, 0.0)
            row_id = lax.broadcasted_iota(jnp.int32, moving.shape, 0)
            col_id = lax.broadcasted_iota(jnp.int32, moving.shape, 1)
            dz = iw[c + BOX_R + 1] - iw[c + BOX_R - 1]
            dy = jnp.where(row_id == rows - 1, 0.0, pltpu.roll(moving, rows - 1, 0)) - jnp.where(
                row_id == 0, 0.0, pltpu.roll(moving, 1, 0)
            )
            dx = jnp.where(col_id == cols - 1, 0.0, pltpu.roll(moving, cols - 1, 1)) - jnp.where(
                col_id == 0, 0.0, pltpu.roll(moving, 1, 1)
            )
            r_ref[0, c] = factor * dz
            r_ref[1, c] = factor * dy
            r_ref[2, c] = factor * dx
            return 0

        lax.fori_loop(0, GROUP, plane, 0)
        return 0

    lax.fori_loop(0, BLOCK // GROUP, group, 0)


def blur_block(b, weights, r_ref, yx, gy, gx, put):
    rows, cols = r_ref.shape[2], r_ref.shape[3]
    base = b * GROUP

    for k in range(3):

        def strip(s, _):
            row = pl.multiple_of(s * STRIP, STRIP)
            for lane in range(0, cols, 128):
                v = [
                    r_ref[k, base + j, pl.ds(row, STRIP), pl.ds(lane, 128)]
                    for j in range(GROUP + 2 * GAUSS_R)
                ]
                for u in range(GROUP):
                    mid = u + GAUSS_R
                    total = weights[0] * v[mid]
                    for o in range(1, GAUSS_R + 1):
                        total = total + weights[o] * (v[mid - o] + v[mid + o])
                    high, low = split2(total)
                    at = u * rows + row
                    yx[k, pl.ds(at, STRIP), pl.ds(lane, 128)] = high
                    yx[k, pl.ds(at, STRIP), pl.ds(cols + lane, 128)] = low
                    yx[k, pl.ds(at, STRIP), pl.ds(2 * cols + lane, 128)] = high
            return 0

        lax.fori_loop(0, rows // STRIP, strip, 0)
    for k in range(3):
        xs = jnp.dot(yx[k], gx[...], preferred_element_type=F32)
        high, low = split2(xs)
        both = jnp.concatenate([high, low, high], axis=0)
        put(k, base, jnp.dot(gy[...], both, preferred_element_type=F32))


def kernel(depth, weights, iw, jw, by, bx, gy, gx, out, loss_out, r_ref, xy, t_ref, yx, loss):
    planes, rows, cols = out.shape[1:]
    z_first = lax.axis_index("gz") * planes
    loss[...] = jnp.zeros_like(loss)
    blocks = -(-(planes + 2 * GAUSS_R) // BLOCK)

    def cov(b, _):
        cov_block(b, z_first, depth, planes, iw, jw, r_ref, xy, t_ref, loss, by, bx)
        return 0

    lax.fori_loop(0, blocks, cov, 0)

    def put(k, base, value):
        out[k, pl.ds(base, GROUP)] = jnp.reshape(value, (GROUP, rows, cols))

    def blur(b, _):
        blur_block(b, weights, r_ref, yx, gy, gx, put)
        return 0

    lax.fori_loop(0, planes // GROUP, blur, 0)
    loss_out[...] = loss[...]


def widened(array, extra):
    size = lax.axis_size("gz")
    up = [(i, i + 1) for i in range(size - 1)]
    down = [(j, i) for i, j in up]
    before = lax.ppermute(array[-HALO:], "gz", up)
    after = lax.ppermute(array[:HALO], "gz", down)
    return jnp.concatenate([before, array, after, jnp.zeros((extra,) + array.shape[1:], F32)])


def on_device(warped):
    moving = warped[0]
    planes, rows, cols = moving.shape
    depth = planes * lax.axis_size("gz")
    by, bx, gy, gx, weights = bands(rows, cols)
    cov_planes = -(-(planes + 2 * GAUSS_R) // BLOCK) * BLOCK
    extra = cov_planes + 2 * BOX_R - planes - 2 * HALO
    template = lax.psum(moving, "subj") / lax.axis_size("subj")
    iw = widened(moving, extra)
    jw = widened(template, extra)
    grows = GROUP * rows
    vmem = pl.BlockSpec(memory_space=pltpu.VMEM)
    force, sims = pl.pallas_call(
        functools.partial(kernel, depth, weights),
        out_shape=(
            jax.ShapeDtypeStruct((3, planes, rows, cols), F32),
            jax.ShapeDtypeStruct((rows, cols), F32),
        ),
        in_specs=[vmem] * 6,
        out_specs=(vmem, vmem),
        scratch_shapes=[
            pltpu.VMEM((3, cov_planes, rows, cols), F32),
            pltpu.VMEM((5, BLOCK // GROUP, 3 * grows, cols), BF16),
            pltpu.VMEM((5, grows, cols), F32),
            pltpu.VMEM((3, grows, 3 * cols), BF16),
            pltpu.VMEM((rows, cols), F32),
        ],
        compiler_params=pltpu.CompilerParams(vmem_limit_bytes=56 * 1024 * 1024),
    )(iw, jw, by, bx, gy, gx)
    loss = -lax.psum(jnp.sum(sims), "gz") / float(depth * rows * cols)
    return (force[None], template, jnp.reshape(loss, (1,)))


def solution(mesh):
    placed = (P("subj", "gz", None, None),)
    return jax.shard_map(
        on_device,
        mesh=mesh,
        in_specs=placed,
        out_specs=(P("subj", None, "gz", None, None), P("gz", None, None), P("subj")),
        check_vma=False,
    )
```

time: 283 us -> 171 us (0.60)
  other arithmetic: 154 us -> 7.75 us
  Pallas kernels: 0 us -> 43.6 us
  waiting for transfers between devices: 79.9 us -> 74.8 us
  local copies, waits for them, and re-layouts: 5.36 us -> 1.4 us
    add x10 -> x0, other arithmetic: 71.2 us -> none  [the longest x2 36.7 us: weighted_sum(): running + weights[offset] * lax.slice_in_dim(padded, offset, offset + pla...]
    pallas_call x0 -> x1, Pallas kernels: none -> 43.6 us  [on_device(): pl.pallas_call(functools.partial(kernel, depth, weights), out_shape=(jax....]
    reduce_sum x1, other arithmetic: 33.1 us -> 1.46 us  [on_device(): loss = -lax.psum(jnp.sum(sims), 'gz') / float(depth * rows * cols)]
    broadcast_in_dim x1 -> x0, other arithmetic: 25.3 us -> none  [on_device(): return (smoothed[None], template, jnp.reshape(loss, (1,)))]
    concatenate x2 -> x1, other arithmetic: 14 us -> 4.46 us  [widened(): jnp.concatenate([before, array, after, jnp.zeros((extra,) + array.shape[1...]
    psum x1, waiting for transfers between devices: 78.7 us -> 70.5 us  [on_device(): template = lax.psum(moving, 'subj') / lax.axis_size('subj')]
    another operation x3 -> x0, other arithmetic: 7.55 us -> none  [local_force(): jnp.stack([factor * slope_depth, factor * slope_rows, factor * slope_cols])]
    unnamed x22 -> x4, local copies, waits for them, and re-layouts: 3.12 us -> 0.01 us
where the time goes in v1:
time: 171 us
  waiting for transfers between devices  74.8 us (44%)
  Pallas kernels  43.6 us (25%)
  blocking collectives  20.8 us (12%)
  between operations  15.9 us (9%)
  other arithmetic  7.75 us (5%)
  starting transfers between devices  6.91 us (4%)
    psum x1, waiting for transfers between devices, on_device(): template = lax.psum(moving, 'subj') / lax.axis_size('subj')  70.5 us
    pallas_call x1, Pallas kernels, on_device(): pl.pallas_call(functools.partial(kernel, depth, weights), out_shape=(jax....  43.6 us
    psum x1, blocking collectives, on_device(): loss = -lax.psum(jnp.sum(sims), 'gz') / float(depth * rows * cols)  20.8 us
    concatenate x1, other arithmetic, widened(): jnp.concatenate([before, array, after, jnp.zeros((extra,) + array.shape[1...  4.46 us
    ppermute x2, starting transfers between devices, widened(): before = lax.ppermute(array[-HALO:], 'gz', up)  4.28 us
    ppermute x2, waiting for transfers between devices, widened(): after = lax.ppermute(array[:HALO], 'gz', down)  3.56 us
  transfers between devices with their start and end apart: 5, of which 2 were waited for; matrix products, arithmetic and copies ran while one was open for 2% of the time, Pallas kernels for 0%

profile of v1, /device:TPU:0, one launch (start us, length us, event | category | flops | bytes accessed | tf_op | source)
XLA Modules:
  0.0 171.1 jit_solution(14386815998811387520)
XLA Ops:
  7.2 0.0 all-reduce.2.cloned.1.call-start
  7.2 0.7 all-reduce.2.cloned.1.call-update
  7.9 1.2 slice_bitcast_fusion.1
  9.1 0.0 copy-start
  9.2 2.5 %collective-permute-start = (f32[7,64,256]{2,1,0:T(8,128)S(1)}, f32[7,64,256]{2,1,0:T(8,128)S(1)}, u32[]{:S(2)}, u32[]{:S(2)}) collective-permute-start(f32[7,64,256]{2,1,0:T(8,128)S(1)} %get-tuple-element.9), channel_id=1, source_target_pairs={{0,1},{1,2},{2,3},{3,4},{4,5},{5,6},{6,7},{8,9},{9,10},{10,11},{11... | collective-permute-start | bytes 1376264 | tf_op jit(solution)/shard_map/ppermute | solution.py:222
  11.7 1.3 collective-permute-start.1
  13.0 70.5 %all-reduce.2.cloned.1.call-done = f32[32,64,256]{2,1,0:T(8,128)} async-done(((f32[32,64,256]{2,1,0:T(8,128)}), f32[32,64,256]{2,1,0:T(8,128)}) %all-reduce.2.cloned.1.call-update) | async-done | bytes 2097168 | tf_op jit(solution)/shard_map/psum | solution.py:234
  83.5 1.8 %broadcast_multiply_fusion = f32[32,64,256]{2,1,0:T(8,128)S(1)} fusion(f32[32,64,256]{2,1,0:T(8,128)} %all-reduce.2.cloned.1.call-done), kind=kLoop, calls=%fused_computation.2 | loop fusion | flops 524288 | bytes 4194304 | tf_op jit(solution)/shard_map/div | solution.py:234
  85.3 0.0 copy-start.1
  85.3 0.1 fusion
  85.4 1.8 %collective-permute-start.2 = (f32[7,64,256]{2,1,0:T(8,128)S(1)}, f32[7,64,256]{2,1,0:T(8,128)S(1)}, u32[]{:S(2)}, u32[]{:S(2)}) collective-permute-start(f32[7,64,256]{2,1,0:T(8,128)S(1)} %get-tuple-element.7), channel_id=1, source_target_pairs={{0,1},{1,2},{2,3},{3,4},{4,5},{5,6},{6,7},{8,9},{9,10},{10,11},{11... | collective-permute-start | bytes 1376264 | tf_op jit(solution)/shard_map/ppermute | solution.py:222
  87.2 1.3 collective-permute-start.3
  88.5 0.1 pad.7.clone
  88.6 0.0 collective-permute-done
  88.6 0.0 collective-permute-done.1
  88.6 0.0 collective-permute-done.2
  88.6 3.6 %collective-permute-done.3 = f32[7,64,256]{2,1,0:T(8,128)S(1)} collective-permute-done((f32[7,64,256]{2,1,0:T(8,128)S(1)}, f32[7,64,256]{2,1,0:T(8,128)S(1)}, u32[]{:S(2)}, u32[]{:S(2)}) %collective-permute-start.3) | collective-permute-done | bytes 458784 | tf_op jit(solution)/shard_map/ppermute | solution.py:223
  92.1 0.0 copy-done
  92.1 4.5 %maximum_maximum_fusion.1 = (f32[48,64,256]{2,1,0:T(8,128)}, f32[48,64,256]{2,1,0:T(8,128)}) fusion(f32[7,64,256]{2,1,0:T(8,128)S(1)} %collective-permute-done.3, f32[32,64,256]{2,1,0:T(8,128)S(1)} %broadcast_multiply_fusion, f32[7,64,256]{2,1,0:T(8,128)S(1)} %collective-permute-done.2, f32[48]{0:T(128)S(1)} %pad.7.clone, ...), kind=kLoop, calls=%fused_computation.1 | loop fusion | flops 4718592 | bytes 12320960 | tf_op jit(solution)/shard_map/concatenate | solution.py:224
  96.6 0.0 copy-done.1
  96.6 43.6 %shard_map.76 = (f32[3,32,64,256]{3,2,1,0:T(8,128)}, f32[64,256]{1,0:T(8,128)}) custom-call(f32[48,64,256]{2,1,0:T(8,128)} %get-tuple-element.12.iw, f32[48,64,256]{2,1,0:T(8,128)} %get-tuple-element.11.jw, bf16[256,768]{1,0:T(8,128)(2,1)} %constant.17.clone.by, bf16[768,256]{1,0:T(8,128)(2,1)} %constant.18.clone.bx, bf16[256,768]{1,0:T(8,128)(2,1)} %constant.19.clone.gy, ...), custom_call_target="tpu_custom_call" | custom-call | tf_op jit(solution)/shard_map/pallas_call | solution.py:239
  140.2 1.5 reduce_sum.9
  141.7 20.8 %psum.15 = f32[]{:T(128)} all-reduce(f32[]{:T(128)} %reduce_sum.9), channel_id=1, replica_groups=mesh['subj'=4,'gz'=8] {'gz'}, use_global_device_ids=true, to_apply=%region_2.0 | all-reduce | flops 1 | bytes 8 | tf_op jit(solution)/shard_map/psum | solution.py:256
  (1 shorter events, 0.0 us)
Async XLA Ops:
  7.2 76.3 %all-reduce.2.cloned.1.call-start = ((), (), s32[]{:S(2)}) async-start(), calls=%async_computation | async-start | bytes 4194304 | tf_op jit(solution)/shard_map/psum | solution.py:234
  9.1 83.0 %copy-start = (f32[1,32,64,256]{3,2,1,0:T(8,128)S(1)}, f32[1,32,64,256]{3,2,1,0:T(8,128)}, u32[]{:S(2)}) copy-start(f32[1,32,64,256]{3,2,1,0:T(8,128)} %param.5) | copy-start | bytes 6291460
  9.2 79.4 %collective-permute-start = (f32[7,64,256]{2,1,0:T(8,128)S(1)}, f32[7,64,256]{2,1,0:T(8,128)S(1)}, u32[]{:S(2)}, u32[]{:S(2)}) collective-permute-start(f32[7,64,256]{2,1,0:T(8,128)S(1)} %get-tuple-element.9), channel_id=1, source_target_pairs={{0,1},{1,2},{2,3},{3,4},{4,5},{5,6},{6,7},{8,9},{9,10},{10,11},{11... | collective-permute-start | bytes 1376264 | tf_op jit(solution)/shard_map/ppermute | solution.py:222
  11.7 76.9 %collective-permute-start.1 = (f32[7,64,256]{2,1,0:T(8,128)S(1)}, f32[7,64,256]{2,1,0:T(8,128)}, u32[]{:S(2)}, u32[]{:S(2)}) collective-permute-start(f32[7,64,256]{2,1,0:T(8,128)S(1)} %get-tuple-element.10), channel_id=1, source_target_pairs={{1,0},{2,1},{3,2},{4,3},{5,4},{6,5},{7,6},{9,8},{10,9},{11,10},{12... | collective-permute-start | bytes 1376264 | tf_op jit(solution)/shard_map/ppermute | solution.py:223
  85.3 11.3 %copy-start.1 = (f32[32,64,256]{2,1,0:T(8,128)}, f32[32,64,256]{2,1,0:T(8,128)S(1)}, u32[]{:S(2)}) copy-start(f32[32,64,256]{2,1,0:T(8,128)S(1)} %broadcast_multiply_fusion) | copy-start | bytes 6291460
  85.4 3.2 %collective-permute-start.2 = (f32[7,64,256]{2,1,0:T(8,128)S(1)}, f32[7,64,256]{2,1,0:T(8,128)S(1)}, u32[]{:S(2)}, u32[]{:S(2)}) collective-permute-start(f32[7,64,256]{2,1,0:T(8,128)S(1)} %get-tuple-element.7), channel_id=1, source_target_pairs={{0,1},{1,2},{2,3},{3,4},{4,5},{5,6},{6,7},{8,9},{9,10},{10,11},{11... | collective-permute-start | bytes 1376264 | tf_op jit(solution)/shard_map/ppermute | solution.py:222
  87.2 5.0 %collective-permute-start.3 = (f32[7,64,256]{2,1,0:T(8,128)S(1)}, f32[7,64,256]{2,1,0:T(8,128)S(1)}, u32[]{:S(2)}, u32[]{:S(2)}) collective-permute-start(f32[7,64,256]{2,1,0:T(8,128)S(1)} %get-tuple-element.8), channel_id=1, source_target_pairs={{1,0},{2,1},{3,2},{4,3},{5,4},{6,5},{7,6},{9,8},{10,9},{11,10},{12... | collective-permute-start | bytes 1376264 | tf_op jit(solution)/shard_map/ppermute | solution.py:223
Sparse Core Ops, SparseCore 0:
  11.1 72.3 all-reduce.1

commit v2 on v1

v2 whole, which is shorter than its diff:
```python
import functools
import math

import jax
import jax.numpy as jnp
import ml_dtypes
import numpy as np
from jax import lax
from jax.experimental import pallas as pl
from jax.experimental.pallas import tpu as pltpu
from jax.sharding import PartitionSpec as P

BOX_R = 4
GAUSS_R = 3
EPS = 1e-05
BLOCK = 8
GROUP = 4
STRIP = 16
F32 = jnp.float32
BF16 = jnp.bfloat16
MESH = pl.DeviceIdType.MESH


def bands(rows, cols):
    bumps = np.array([math.exp(-(k * k) / 8.0) for k in range(-GAUSS_R, GAUSS_R + 1)])
    bumps = bumps / bumps.sum()

    def band(n, weights, radius):
        out = np.zeros((n, n), np.float32)
        for k in range(-radius, radius + 1):
            out += np.diag(np.full(n - abs(k), weights[k + radius], np.float32), k)
        return out

    def high_low(m):
        high = m.astype(ml_dtypes.bfloat16)
        low = (m - high.astype(np.float32)).astype(ml_dtypes.bfloat16)
        return high, low

    ones = np.ones(2 * BOX_R + 1)
    eye = np.eye(GROUP, dtype=np.float32)
    box_y = np.kron(eye, band(rows, ones, BOX_R)).astype(ml_dtypes.bfloat16)
    box_x = band(cols, ones, BOX_R).astype(ml_dtypes.bfloat16)
    gy_high, gy_low = high_low(np.kron(eye, band(rows, bumps, GAUSS_R)))
    gx_high, gx_low = high_low(band(cols, bumps, GAUSS_R))
    return (
        np.concatenate([box_y] * 3, axis=1),
        np.concatenate([box_x] * 3, axis=0),
        np.concatenate([gy_high, gy_high, gy_low], axis=1),
        np.concatenate([gx_high, gx_high, gx_low], axis=0),
        [float(b) for b in bumps[GAUSS_R:]],
    )


def split3(v):
    a = v.astype(BF16)
    r = v - a.astype(F32)
    b = r.astype(BF16)
    c = (r - b.astype(F32)).astype(BF16)
    return a, b, c


def split2(v):
    a = v.astype(BF16)
    return a, (v - a.astype(F32)).astype(BF16)


def windows(planes):
    n = BLOCK
    span = 2 * BOX_R + 1
    head = [None] * (n + 1)
    acc = planes[n - 1]
    head[n - 1] = acc
    for i in range(n - 2, -1, -1):
        acc = acc + planes[i]
        head[i] = acc
    out = []
    tail = None
    for i in range(n):
        tail = planes[n + i] if tail is None else tail + planes[n + i]
        out.append(head[i] + tail)
    assert span == n + 1
    return out


def box_block(b, first, count, iw, jw, xy, t_ref, by, bx):
    rows, cols = iw.shape[1], iw.shape[2]
    base = b * BLOCK
    grows = GROUP * rows
    span = BLOCK + 2 * BOX_R

    def strip(s, _):
        row = pl.multiple_of(s * STRIP, STRIP)
        for lane in range(0, cols, 128):
            iv = [iw[base + k, pl.ds(row, STRIP), pl.ds(lane, 128)] for k in range(span)]
            if first + count > 2:
                jv = [jw[base + k, pl.ds(row, STRIP), pl.ds(lane, 128)] for k in range(span)]
            for v in range(first, first + count):
                if v == 0:
                    vol = iv
                elif v == 1:
                    vol = [a * a for a in iv]
                elif v == 2:
                    vol = jv
                elif v == 3:
                    vol = [a * a for a in jv]
                else:
                    vol = [a * c for a, c in zip(iv, jv)]
                for w, total in enumerate(windows(vol)):
                    g, u = w // GROUP, w % GROUP
                    for k, piece in enumerate(split3(total)):
                        at = k * grows + u * rows
                        xy[v - first, g, pl.ds(at + row, STRIP), pl.ds(lane, 128)] = piece
        return 0

    lax.fori_loop(0, rows // STRIP, strip, 0)

    def group(g, _):
        at = pl.multiple_of(b * BLOCK * rows + g * grows, grows)
        for v in range(count):
            ys = jnp.dot(by[...], xy[v, g], preferred_element_type=F32)
            xs = jnp.concatenate(split3(ys), axis=1)
            t_ref[first + v, pl.ds(at, grows), :] = jnp.dot(
                xs, bx[...], preferred_element_type=F32
            )
        return 0

    lax.fori_loop(0, BLOCK // GROUP, group, 0)


def force_block(b, z_first, depth, planes, iw, jw, r_ref, t_ref, loss):
    rows, cols = iw.shape[1], iw.shape[2]
    scale = 1.0 / float((2 * BOX_R + 1) ** 3)

    def plane(u, _):
        c = b * BLOCK + u
        at = pl.multiple_of(c * rows, rows)
        m = [t_ref[v, pl.ds(at, rows), :] * scale for v in range(5)]
        mi, mj = m[0], m[2]
        var_i = m[1] - mi * mi
        var_j = m[3] - mj * mj
        cc = m[4] - mi * mj
        moving = iw[c + BOX_R]
        target = jw[c + BOX_R]
        q = cc / (var_i * var_j + EPS)
        core = c - BOX_R
        z = z_first + core
        owned = jnp.logical_and(core >= 0, core < planes)
        loss[...] += jnp.where(owned, cc * q, 0.0)
        factor = q * ((target - mj) - cc / (var_i + EPS) * (moving - mi))
        inside = jnp.logical_and(z >= 0, z < depth)
        factor = jnp.where(inside, factor, 0.0)
        row_id = lax.broadcasted_iota(jnp.int32, moving.shape, 0)
        col_id = lax.broadcasted_iota(jnp.int32, moving.shape, 1)
        dz = iw[c + BOX_R + 1] - iw[c + BOX_R - 1]
        dy = jnp.where(row_id == rows - 1, 0.0, pltpu.roll(moving, rows - 1, 0)) - jnp.where(
            row_id == 0, 0.0, pltpu.roll(moving, 1, 0)
        )
        dx = jnp.where(col_id == cols - 1, 0.0, pltpu.roll(moving, cols - 1, 1)) - jnp.where(
            col_id == 0, 0.0, pltpu.roll(moving, 1, 1)
        )
        r_ref[0, c] = factor * dz
        r_ref[1, c] = factor * dy
        r_ref[2, c] = factor * dx
        return 0

    lax.fori_loop(0, BLOCK, plane, 0)


def blur_block(b, weights, r_ref, yx, gy, gx, put):
    rows, cols = r_ref.shape[2], r_ref.shape[3]
    base = b * GROUP

    for k in range(3):

        def strip(s, _):
            row = pl.multiple_of(s * STRIP, STRIP)
            for lane in range(0, cols, 128):
                v = [
                    r_ref[k, base + BOX_R - GAUSS_R + j, pl.ds(row, STRIP), pl.ds(lane, 128)]
                    for j in range(GROUP + 2 * GAUSS_R)
                ]
                for u in range(GROUP):
                    mid = u + GAUSS_R
                    total = weights[0] * v[mid]
                    for o in range(1, GAUSS_R + 1):
                        total = total + weights[o] * (v[mid - o] + v[mid + o])
                    high, low = split2(total)
                    at = u * rows + row
                    yx[k, pl.ds(at, STRIP), pl.ds(lane, 128)] = high
                    yx[k, pl.ds(at, STRIP), pl.ds(cols + lane, 128)] = low
                    yx[k, pl.ds(at, STRIP), pl.ds(2 * cols + lane, 128)] = high
            return 0

        lax.fori_loop(0, rows // STRIP, strip, 0)
    for k in range(3):
        xs = jnp.dot(yx[k], gx[...], preferred_element_type=F32)
        high, low = split2(xs)
        both = jnp.concatenate([high, low, high], axis=0)
        put(k, base, jnp.dot(gy[...], both, preferred_element_type=F32))


def kernel(
    shape, weights, x, by, bx, gy, gx, out, template, loss_out,
    iw, jw, part, got, r_ref, xy, t_ref, yx, out_v, loss, loss_all,
    load_sem, ar_send, ar_recv, halo_send, halo_recv, loss_send, loss_recv, put_sem,
):
    members, size = shape
    planes, rows, cols = x.shape[1:]
    bits = members.bit_length() - 1
    chunks = planes // BLOCK
    stages = 2 * bits - 1
    me = lax.axis_index("subj")
    gz = lax.axis_index("gz")
    z_first, depth = gz * planes, planes * size
    has_low, has_high = gz > 0, gz < size - 1

    def flip(bit):
        mine = (me // (1 << bit)) % 2
        return mine, me + (1 - 2 * mine) * (1 << bit)

    barrier = pltpu.get_barrier_semaphore()
    for bit in range(bits):
        pl.semaphore_signal(barrier, inc=1, device_id={"subj": flip(bit)[1]}, device_id_type=MESH)
    for d in range(1, size):
        peer = lax.rem(gz + d, size)
        pl.semaphore_signal(barrier, inc=1, device_id={"gz": peer}, device_id_type=MESH)

    loads = [
        pltpu.make_async_copy(
            x.at[0, pl.ds(c * BLOCK, BLOCK)], iw.at[pl.ds((c + 1) * BLOCK, BLOCK)], load_sem.at[c]
        )
        for c in range(chunks)
    ]
    for load in loads:
        load.start()
    pl.semaphore_wait(barrier, bits + size - 1)

    half = rows // 2
    plans = []
    for h in range(2):
        order = list(range(bits)) if h == 0 else list(range(bits))[::-1]
        at, length, levels = h * half, half, []
        for bit in order[:-1]:
            mine, peer = flip(bit)
            length //= 2
            kept = at + mine * length
            levels.append((peer, kept, at + (1 - mine) * length, length))
            at = kept
        levels.append((flip(order[-1])[1], at, at, length))
        plans.append(levels)

    def ds(at, length):
        return pl.ds(pl.multiple_of(at, length), length)

    def step(s, h, c):
        deep = s if s < bits else stages - 1 - s
        peer, kept, sent, length = plans[h][deep]
        wide = pl.ds((c + 1) * BLOCK, BLOCK)
        if s >= bits:
            src = jw.at[wide, ds(kept, length)]
            dst = src
        else:
            if s == 0:
                src = x.at[0, pl.ds(c * BLOCK, BLOCK), ds(sent, length)]
            else:
                above = plans[h][s - 1][1]
                src = part.at[s - 1, h, pl.ds(c * BLOCK, BLOCK), ds(sent - above, length)]
            dst = got.at[s, h, pl.ds(c * BLOCK, BLOCK), pl.ds(0, length)]
        return pltpu.make_async_remote_copy(
            src_ref=src,
            dst_ref=dst,
            send_sem=ar_send.at[s, h, c],
            recv_sem=ar_recv.at[s, h, c],
            device_id={"subj": peer},
            device_id_type=MESH,
        )

    def finish(s, c):
        if s == 0:
            loads[c].wait()
        for h in range(2):
            step(s, h, c).wait_recv()
            if s < bits:
                peer, kept, sent, length = plans[h][s]
                here = pl.ds(c * BLOCK, BLOCK)
                new = got[s, h, here, pl.ds(0, length), :]
                if s == 0:
                    old = iw[pl.ds((c + 1) * BLOCK, BLOCK), ds(kept, length), :]
                else:
                    above = plans[h][s - 1][1]
                    old = part[s - 1, h, here, ds(kept - above, length), :]
                if s < bits - 1:
                    part[s, h, here, pl.ds(0, length), :] = old + new
                else:
                    jw[pl.ds((c + 1) * BLOCK, BLOCK), ds(kept, length), :] = (old + new) / members
            if s + 1 < stages:
                step(s + 1, h, c).start()
        if s == stages - 1:
            if c == 0:
                halo(1, 0, 0, "start")
            if c == chunks - 1:
                halo(1, 1, 0, "start")
            pltpu.make_async_copy(
                jw.at[pl.ds((c + 1) * BLOCK, BLOCK)],
                template.at[pl.ds(c * BLOCK, BLOCK)],
                put_sem.at[planes // GROUP + c],
            ).start()

    def halo(which, way, recv, what):
        core = 0 if way == 0 else planes - BLOCK
        there = planes + BLOCK if way == 0 else 0
        wide = iw if which == 0 else jw
        if which == 0:
            src = x.at[0, pl.ds(core, BLOCK)]
        else:
            src = jw.at[pl.ds(core + BLOCK, BLOCK)]
        peer = gz - 1 if way == 0 else gz + 1
        can_send = has_low if way == 0 else has_high
        can_take = has_high if way == 0 else has_low
        copy = pltpu.make_async_remote_copy(
            src_ref=src,
            dst_ref=wide.at[pl.ds(there, BLOCK)],
            send_sem=halo_send.at[which, way],
            recv_sem=halo_recv.at[which, way],
            device_id={"gz": lax.rem(peer + size, size)},
            device_id_type=MESH,
        )

        @pl.when(can_take if recv else can_send)
        def _():
            if what == "start":
                copy.start()
            elif recv:
                copy.wait_recv()
            else:
                copy.wait_send()

    for c in range(chunks):
        for h in range(2):
            step(0, h, c).start()
    halo(0, 0, 0, "start")
    halo(0, 1, 0, "start")

    nothing = jnp.zeros((BLOCK, rows, cols), F32)

    @pl.when(jnp.logical_not(has_low))
    def _():
        iw[pl.ds(0, BLOCK)] = nothing
        jw[pl.ds(0, BLOCK)] = nothing

    @pl.when(jnp.logical_not(has_high))
    def _():
        iw[pl.ds(planes + BLOCK, BLOCK)] = nothing
        jw[pl.ds(planes + BLOCK, BLOCK)] = nothing

    loss[...] = jnp.zeros_like(loss)
    blocks = chunks + 1
    work = [(s, c) for s in range(stages - 1) for c in range(chunks)]

    def pick(i):
        return jnp.where(i < chunks - 1, i + 1, (i - chunks + 1) * chunks)

    def moving_part(i, _):
        for slot in range(blocks):
            todo = [w for j, w in enumerate(work) if j * (blocks + 1) // len(work) == slot]

            @pl.when(i == slot)
            def _(todo=todo, slot=slot):
                for s, c in todo:
                    finish(s, c)
                if slot == chunks - 1:
                    halo(0, 1, 1, "wait")
                if slot == chunks:
                    halo(0, 0, 1, "wait")

        box_block(pick(i), 0, 2, iw, jw, xy, t_ref, by, bx)
        return 0

    lax.fori_loop(0, blocks, moving_part, 0)
    for j, (s, c) in enumerate(work):
        if j * (blocks + 1) // len(work) == blocks:
            finish(s, c)

    def target_part(i, _):
        for slot in range(blocks):

            @pl.when(i == slot)
            def _(slot=slot):
                if slot == 0:
                    finish(stages - 1, 0)
                if slot + 1 < chunks:
                    finish(stages - 1, slot + 1)
                if slot == chunks - 1:
                    halo(1, 1, 1, "wait")
                if slot == chunks:
                    halo(1, 0, 1, "wait")

        b = pick(i)
        box_block(b, 2, 3, iw, jw, xy, t_ref, by, bx)
        force_block(b, z_first, depth, planes, iw, jw, r_ref, t_ref, loss)
        return 0

    lax.fori_loop(0, blocks, target_part, 0)

    total = jnp.zeros((8, 128), F32)
    for row in range(0, rows, 8):
        for lane in range(0, cols, 128):
            total = total + loss[pl.ds(row, 8), pl.ds(lane, 128)]
    loss_all[gz] = total

    def share(d):
        return pltpu.make_async_remote_copy(
            src_ref=loss_all.at[gz],
            dst_ref=loss_all.at[gz],
            send_sem=loss_send.at[d],
            recv_sem=loss_recv.at[d],
            device_id={"gz": lax.rem(gz + d, size)},
            device_id_type=MESH,
        )

    for d in range(1, size):
        share(d).start()

    def put(k, base, value):
        out_v[k, pl.ds(base, GROUP)] = jnp.reshape(value, (GROUP, rows, cols))

    def put_copy(g):
        at = pl.ds(g * GROUP, GROUP)
        return pltpu.make_async_copy(out_v.at[:, at], out.at[0, :, at], put_sem.at[g])

    def blur(g, _):
        blur_block(g, weights, r_ref, yx, gy, gx, put)
        put_copy(g).start()
        return 0

    lax.fori_loop(0, planes // GROUP, blur, 0)

    for d in range(1, size):
        share(d).wait_recv()
    sims = loss_all[0]
    for k in range(1, size):
        sims = sims + loss_all[k]
    loss_out[0] = -jnp.sum(sims) / float(depth * rows * cols)

    for g in range(planes // GROUP):
        put_copy(g).wait()
    for c in range(chunks):
        pltpu.make_async_copy(
            jw.at[pl.ds((c + 1) * BLOCK, BLOCK)],
            template.at[pl.ds(c * BLOCK, BLOCK)],
            put_sem.at[planes // GROUP + c],
        ).wait()
    for d in range(1, size):
        share(d).wait_send()
    for s in range(stages):
        for h in range(2):
            for c in range(chunks):
                step(s, h, c).wait_send()
    for which in range(2):
        for way in range(2):
            halo(which, way, 0, "wait")


def on_device(warped):
    planes, rows, cols = warped.shape[1:]
    members, size = lax.axis_size("subj"), lax.axis_size("gz")
    bits = members.bit_length() - 1
    assert members == 1 << bits and bits > 1 and planes % BLOCK == 0
    by, bx, gy, gx, weights = bands(rows, cols)
    chunks = planes // BLOCK
    stages = 2 * bits - 1
    grows = GROUP * rows
    vmem = pl.BlockSpec(memory_space=pltpu.VMEM)
    anywhere = pl.BlockSpec(memory_space=pl.ANY)
    cells = planes * rows * cols
    dma = pltpu.SemaphoreType.DMA
    force, template, loss = pl.pallas_call(
        functools.partial(kernel, (members, size), weights),
        out_shape=(
            jax.ShapeDtypeStruct((1, 3, planes, rows, cols), F32),
            jax.ShapeDtypeStruct((planes, rows, cols), F32),
            jax.ShapeDtypeStruct((1,), F32),
        ),
        in_specs=[anywhere] + [vmem] * 4,
        out_specs=(anywhere, anywhere, pl.BlockSpec(memory_space=pltpu.SMEM)),
        scratch_shapes=[
            pltpu.VMEM((planes + 2 * BLOCK, rows, cols), F32),
            pltpu.VMEM((planes + 2 * BLOCK, rows, cols), F32),
            pltpu.VMEM((bits - 1, 2, planes, rows // 4, cols), F32),
            pltpu.VMEM((bits, 2, planes, rows // 4, cols), F32),
            pltpu.VMEM((3, planes + BLOCK, rows, cols), F32),
            pltpu.VMEM((3, BLOCK // GROUP, 3 * grows, cols), BF16),
            pltpu.VMEM((5, (planes + BLOCK) * rows, cols), F32),
            pltpu.VMEM((3, grows, 3 * cols), BF16),
            pltpu.VMEM((3, planes, rows, cols), F32),
            pltpu.VMEM((rows, cols), F32),
            pltpu.VMEM((size, 8, 128), F32),
            dma((chunks,)),
            dma((stages, 2, chunks)),
            dma((stages, 2, chunks)),
            dma((2, 2)),
            dma((2, 2)),
            dma((size,)),
            dma((size,)),
            dma((planes // GROUP + chunks,)),
        ],
        compiler_params=pltpu.CompilerParams(
            collective_id=0, has_side_effects=True, vmem_limit_bytes=60 * 1024 * 1024
        ),
        cost_estimate=pl.CostEstimate(
            flops=300 * cells, bytes_accessed=20 * cells, transcendentals=0
        ),
    )(warped, by, bx, gy, gx)
    return (force, template, loss)


def solution(mesh):
    placed = (P("subj", "gz", None, None),)
    return jax.shard_map(
        on_device,
        mesh=mesh,
        in_specs=placed,
        out_specs=(P("subj", None, "gz", None, None), P("gz", None, None), P("subj")),
        check_vma=False,
    )
```

time: 171 us -> 82.3 us (0.48)
  waiting for transfers between devices: 74.8 us -> 0 us
  Pallas kernels: 43.6 us -> 71.1 us
  blocking collectives: 20.8 us -> 0 us
  between operations: 15.9 us -> 2.35 us
  other arithmetic: 7.75 us -> 0 us
  starting transfers between devices: 6.91 us -> 0 us
  local copies, waits for them, and re-layouts: 1.4 us -> 7.77 us
    psum x1 -> x0, waiting for transfers between devices: 70.5 us -> none  [on_device(): template = lax.psum(moving, 'subj') / lax.axis_size('subj')]
    pallas_call x1, Pallas kernels: 43.6 us -> 71.1 us  [on_device(): pl.pallas_call(functools.partial(kernel, (members, size), weights), out_s...]
    psum x1 -> x0, blocking collectives: 20.8 us -> none  [on_device(): loss = -lax.psum(jnp.sum(sims), 'gz') / float(depth * rows * cols)]
    unnamed x4, local copies, waits for them, and re-layouts: 0.01 us -> 7.77 us
    ppermute x4 -> x0, starting transfers between devices: 6.87 us -> none  [the longest x2 4.28 us: widened(): before = lax.ppermute(array[-HALO:], 'gz', up)]
    concatenate x1 -> x0, other arithmetic: 4.46 us -> none  [widened(): jnp.concatenate([before, array, after, jnp.zeros((extra,) + array.shape[1...]
    ppermute x4 -> x0, waiting for transfers between devices: 3.57 us -> none  [the longest x2 3.56 us: widened(): after = lax.ppermute(array[:HALO], 'gz', down)]
    div x1 -> x0, other arithmetic: 1.83 us -> none  [on_device(): template = lax.psum(moving, 'subj') / lax.axis_size('subj')]
  transfers between devices with their start and end apart: 5 -> 0, of which waited for: 2 -> 0; matrix products, arithmetic and copies ran while one was open for 2% -> 0% of each run, Pallas kernels for 0% -> 0%
where the time goes in v2:
time: 82.3 us; the launch traced here: 81.2 us
  Pallas kernels  71.1 us (86%)
  local copies, waits for them, and re-layouts  7.77 us (9%)
  between operations  2.35 us (3%)
    pallas_call x1, Pallas kernels, on_device(): pl.pallas_call(functools.partial(kernel, (members, size), weights), out_s...  71.1 us
    unnamed x4, local copies, waits for them, and re-layouts  7.77 us

profile of v2, /device:TPU:0, one launch (start us, length us, event | category | flops | bytes accessed | tf_op | source)
XLA Modules:
  0.0 81.2 jit_solution(10784641754560183963)
XLA Ops:
  0.6 71.1 %shard_map.76 = (f32[1,3,32,64,256]{4,3,2,1,0:T(8,128)}, f32[32,64,256]{2,1,0:T(8,128)}, f32[1]{0:T(128)}) custom-call(f32[1,32,64,256]{3,2,1,0:T(8,128)} %x.1, bf16[256,768]{1,0:T(8,128)(2,1)} %constant.8.clone.by, bf16[768,256]{1,0:T(8,128)(2,1)} %constant.9.clone.bx, bf16[256,768]{1,0:T(8,128)(2,1)} %constant.10.clone.gy, bf16[768,256]{1,0:T(8,128)(2,1)} %constant.11.clone.gx), custom_call_target="tpu_custom_call" | custom-call | flops 157286400 | bytes 10485760 | tf_op jit(solution)/shard_map/pallas_call | solution.py:477
  71.7 0.0 copy-start
  71.8 6.4 %copy.11 = f32[1,3,32,64,256]{4,3,2,1,0:T(8,128)} copy(f32[1,3,32,64,256]{4,3,2,1,0:T(8,128)} %get-tuple-element.6) | data formatting | bytes 12582912
  78.2 0.0 copy-done
  78.2 1.3 %copy.12 = f32[32,64,256]{2,1,0:T(8,128)} copy(f32[32,64,256]{2,1,0:T(8,128)S(1)} %copy-done) | data formatting | bytes 4194304
Async XLA Ops:
  71.7 6.5 %copy-start = (f32[32,64,256]{2,1,0:T(8,128)S(1)}, f32[32,64,256]{2,1,0:T(8,128)}, u32[]{:S(2)}) copy-start(f32[32,64,256]{2,1,0:T(8,128)} %get-tuple-element.7) | copy-start | bytes 6291460

commit v3 on v2

--- a/solution.py
+++ b/solution.py
@@ -16,6 +16,7 @@
 BLOCK = 8
 GROUP = 4
 STRIP = 16
+PIECE = 4
 F32 = jnp.float32
 BF16 = jnp.bfloat16
 MESH = pl.DeviceIdType.MESH
@@ -200,14 +201,15 @@
 
 
 def kernel(
-    shape, weights, x, by, bx, gy, gx, out, template, loss_out,
-    iw, jw, part, got, r_ref, xy, t_ref, yx, out_v, loss, loss_all,
+    shape, x, by, bx, raw, template, loss_out,
+    iw, jw, part, got, r_ref, xy, t_ref, loss, loss_all,
     load_sem, ar_send, ar_recv, halo_send, halo_recv, loss_send, loss_recv, put_sem,
 ):
     members, size = shape
     planes, rows, cols = x.shape[1:]
     bits = members.bit_length() - 1
     chunks = planes // BLOCK
+    pieces = planes // PIECE
     stages = 2 * bits - 1
     me = lax.axis_index("subj")
     gz = lax.axis_index("gz")
@@ -255,17 +257,17 @@
     def step(s, h, c):
         deep = s if s < bits else stages - 1 - s
         peer, kept, sent, length = plans[h][deep]
-        wide = pl.ds((c + 1) * BLOCK, BLOCK)
+        wide = pl.ds(BLOCK + c * PIECE, PIECE)
         if s >= bits:
             src = jw.at[wide, ds(kept, length)]
             dst = src
         else:
             if s == 0:
-                src = x.at[0, pl.ds(c * BLOCK, BLOCK), ds(sent, length)]
+                src = x.at[0, pl.ds(c * PIECE, PIECE), ds(sent, length)]
             else:
                 above = plans[h][s - 1][1]
-                src = part.at[s - 1, h, pl.ds(c * BLOCK, BLOCK), ds(sent - above, length)]
-            dst = got.at[s, h, pl.ds(c * BLOCK, BLOCK), pl.ds(0, length)]
+                src = part.at[s - 1, h, pl.ds(c * PIECE, PIECE), ds(sent - above, length)]
+            dst = got.at[s, h, pl.ds(c * PIECE, PIECE), pl.ds(0, length)]
         return pltpu.make_async_remote_copy(
             src_ref=src,
             dst_ref=dst,
@@ -276,35 +278,24 @@
         )
 
     def finish(s, c):
-        if s == 0:
-            loads[c].wait()
         for h in range(2):
             step(s, h, c).wait_recv()
             if s < bits:
                 peer, kept, sent, length = plans[h][s]
-                here = pl.ds(c * BLOCK, BLOCK)
+                here = pl.ds(c * PIECE, PIECE)
+                core = pl.ds(BLOCK + c * PIECE, PIECE)
                 new = got[s, h, here, pl.ds(0, length), :]
                 if s == 0:
-                    old = iw[pl.ds((c + 1) * BLOCK, BLOCK), ds(kept, length), :]
+                    old = iw[core, ds(kept, length), :]
                 else:
                     above = plans[h][s - 1][1]
                     old = part[s - 1, h, here, ds(kept - above, length), :]
                 if s < bits - 1:
                     part[s, h, here, pl.ds(0, length), :] = old + new
                 else:
-                    jw[pl.ds((c + 1) * BLOCK, BLOCK), ds(kept, length), :] = (old + new) / members
+                    jw[core, ds(kept, length), :] = (old + new) / members
             if s + 1 < stages:
                 step(s + 1, h, c).start()
-        if s == stages - 1:
-            if c == 0:
-                halo(1, 0, 0, "start")
-            if c == chunks - 1:
-                halo(1, 1, 0, "start")
-            pltpu.make_async_copy(
-                jw.at[pl.ds((c + 1) * BLOCK, BLOCK)],
-                template.at[pl.ds(c * BLOCK, BLOCK)],
-                put_sem.at[planes // GROUP + c],
-            ).start()
 
     def halo(which, way, recv, what):
         core = 0 if way == 0 else planes - BLOCK
@@ -335,9 +326,18 @@
             else:
                 copy.wait_send()
 
-    for c in range(chunks):
-        for h in range(2):
-            step(0, h, c).start()
+    edge = BLOCK // PIECE
+    order = list(range(edge)) + list(range(pieces - edge, pieces))
+    order += list(range(edge, pieces - edge))
+    ahead = 4
+
+    def first(pos):
+        if pos < pieces:
+            for h in range(2):
+                step(0, h, order[pos]).start()
+
+    for pos in range(ahead):
+        first(pos)
     halo(0, 0, 0, "start")
     halo(0, 1, 0, "start")
 
@@ -355,52 +355,85 @@
 
     loss[...] = jnp.zeros_like(loss)
     blocks = chunks + 1
-    work = [(s, c) for s in range(stages - 1) for c in range(chunks)]
-
-    def pick(i):
-        return jnp.where(i < chunks - 1, i + 1, (i - chunks + 1) * chunks)
+    last = 2 * (stages - 1)
+    events = sorted((pos + 2 * s, -s, pos) for s in range(stages) for pos in range(pieces))
+
+    def need(slot):
+        b = 0 if slot == 0 else chunks if slot == 1 else slot - 1
+        cells = [c for c in range((b - 1) * edge, (b + 1) * edge) if 0 <= c < pieces]
+        return last + max(order.index(c) for c in cells)
+
+    def place(key):
+        if key < last + 2:
+            return 0, key * blocks // (last + 2)
+        if key <= last + 2 * edge - 1:
+            return 1, 0
+        if key == last + 2 * edge:
+            return 2, 0
+        if key == last + 2 * edge + 1:
+            return 1, 1
+        return 1, min(t for t in range(blocks) if need(t) >= key)
+
+    def serve(kind, slot):
+        for key, s, pos in events:
+            if place(key) == (kind, slot):
+                finish(-s, order[pos])
+                if s == 0:
+                    first(pos + ahead)
+                if -s == stages - 1 and pos == edge - 1:
+                    halo(1, 0, 0, "start")
+                if -s == stages - 1 and pos == 2 * edge - 1:
+                    halo(1, 1, 0, "start")
+
+    for load in loads:
+        load.wait()
 
     def moving_part(i, _):
         for slot in range(blocks):
-            todo = [w for j, w in enumerate(work) if j * (blocks + 1) // len(work) == slot]
 
             @pl.when(i == slot)
-            def _(todo=todo, slot=slot):
-                for s, c in todo:
-                    finish(s, c)
+            def _(slot=slot):
+                serve(0, slot)
                 if slot == chunks - 1:
                     halo(0, 1, 1, "wait")
                 if slot == chunks:
                     halo(0, 0, 1, "wait")
 
-        box_block(pick(i), 0, 2, iw, jw, xy, t_ref, by, bx)
+        b = jnp.where(i < chunks - 1, i + 1, (i - chunks + 1) * chunks)
+        box_block(b, 0, 2, iw, jw, xy, t_ref, by, bx)
         return 0
 
     lax.fori_loop(0, blocks, moving_part, 0)
-    for j, (s, c) in enumerate(work):
-        if j * (blocks + 1) // len(work) == blocks:
-            finish(s, c)
+
+    def raw_copy(b):
+        at = pl.ds(b * BLOCK, BLOCK)
+        return pltpu.make_async_copy(r_ref.at[:, at], raw.at[:, at], put_sem.at[b])
 
     def target_part(i, _):
         for slot in range(blocks):
 
             @pl.when(i == slot)
             def _(slot=slot):
+                serve(1, slot)
                 if slot == 0:
-                    finish(stages - 1, 0)
-                if slot + 1 < chunks:
-                    finish(stages - 1, slot + 1)
-                if slot == chunks - 1:
                     halo(1, 1, 1, "wait")
-                if slot == chunks:
+                if slot == 1:
                     halo(1, 0, 1, "wait")
 
-        b = pick(i)
+        b = jnp.where(i == 0, 0, jnp.where(i == 1, chunks, i - 1))
         box_block(b, 2, 3, iw, jw, xy, t_ref, by, bx)
+
+        @pl.when(i == 0)
+        def _():
+            serve(2, 0)
+
         force_block(b, z_first, depth, planes, iw, jw, r_ref, t_ref, loss)
+        raw_copy(b).start()
         return 0
 
     lax.fori_loop(0, blocks, target_part, 0)
+    whole = pltpu.make_async_copy(jw.at[pl.ds(BLOCK, planes)], template, put_sem.at[blocks])
+    whole.start()
 
     total = jnp.zeros((8, 128), F32)
     for row in range(0, rows, 8):
@@ -421,20 +454,6 @@
     for d in range(1, size):
         share(d).start()
 
-    def put(k, base, value):
-        out_v[k, pl.ds(base, GROUP)] = jnp.reshape(value, (GROUP, rows, cols))
-
-    def put_copy(g):
-        at = pl.ds(g * GROUP, GROUP)
-        return pltpu.make_async_copy(out_v.at[:, at], out.at[0, :, at], put_sem.at[g])
-
-    def blur(g, _):
-        blur_block(g, weights, r_ref, yx, gy, gx, put)
-        put_copy(g).start()
-        return 0
-
-    lax.fori_loop(0, planes // GROUP, blur, 0)
-
     for d in range(1, size):
         share(d).wait_recv()
     sims = loss_all[0]
@@ -442,23 +461,54 @@
         sims = sims + loss_all[k]
     loss_out[0] = -jnp.sum(sims) / float(depth * rows * cols)
 
-    for g in range(planes // GROUP):
-        put_copy(g).wait()
-    for c in range(chunks):
-        pltpu.make_async_copy(
-            jw.at[pl.ds((c + 1) * BLOCK, BLOCK)],
-            template.at[pl.ds(c * BLOCK, BLOCK)],
-            put_sem.at[planes // GROUP + c],
-        ).wait()
+    for b in range(blocks):
+        raw_copy(b).wait()
+    whole.wait()
     for d in range(1, size):
         share(d).wait_send()
     for s in range(stages):
         for h in range(2):
-            for c in range(chunks):
+            for c in range(pieces):
                 step(s, h, c).wait_send()
     for which in range(2):
         for way in range(2):
             halo(which, way, 0, "wait")
+
+
+def blur_kernel(weights, raw, mean, gy, gx, out, template, r_ref, yx, out_v, load_sem, put_sem):
+    planes, rows, cols = out.shape[2:]
+    blocks = raw.shape[1] // BLOCK
+
+    def load(b):
+        at = pl.ds(b * BLOCK, BLOCK)
+        return pltpu.make_async_copy(raw.at[:, at], r_ref.at[:, at], load_sem.at[b])
+
+    for b in range(blocks):
+        load(b).start()
+    whole = pltpu.make_async_copy(mean, template, load_sem.at[blocks])
+    whole.start()
+    load(0).wait()
+
+    def put(k, base, value):
+        out_v[k, pl.ds(base, GROUP)] = jnp.reshape(value, (GROUP, rows, cols))
+
+    def put_copy(g):
+        at = pl.ds(g * GROUP, GROUP)
+        return pltpu.make_async_copy(out_v.at[:, at], out.at[0, :, at], put_sem.at[g])
+
+    def blur(g, _):
+        @pl.when(lax.rem(g, BLOCK // GROUP) == 0)
+        def _():
+            load(g // (BLOCK // GROUP) + 1).wait()
+
+        blur_block(g, weights, r_ref, yx, gy, gx, put)
+        put_copy(g).start()
+        return 0
+
+    lax.fori_loop(0, planes // GROUP, blur, 0)
+    for g in range(planes // GROUP):
+        put_copy(g).wait()
+    whole.wait()
 
 
 def on_device(warped):
@@ -467,50 +517,69 @@
     bits = members.bit_length() - 1
     assert members == 1 << bits and bits > 1 and planes % BLOCK == 0
     by, bx, gy, gx, weights = bands(rows, cols)
-    chunks = planes // BLOCK
+    chunks, pieces = planes // BLOCK, planes // PIECE
     stages = 2 * bits - 1
     grows = GROUP * rows
     vmem = pl.BlockSpec(memory_space=pltpu.VMEM)
     anywhere = pl.BlockSpec(memory_space=pl.ANY)
     cells = planes * rows * cols
     dma = pltpu.SemaphoreType.DMA
-    force, template, loss = pl.pallas_call(
-        functools.partial(kernel, (members, size), weights),
+    raw_shape = (3, planes + BLOCK, rows, cols)
+    raw, mean, loss = pl.pallas_call(
+        functools.partial(kernel, (members, size)),
         out_shape=(
-            jax.ShapeDtypeStruct((1, 3, planes, rows, cols), F32),
+            jax.ShapeDtypeStruct(raw_shape, F32),
             jax.ShapeDtypeStruct((planes, rows, cols), F32),
             jax.ShapeDtypeStruct((1,), F32),
         ),
-        in_specs=[anywhere] + [vmem] * 4,
+        in_specs=[anywhere] + [vmem] * 2,
         out_specs=(anywhere, anywhere, pl.BlockSpec(memory_space=pltpu.SMEM)),
         scratch_shapes=[
             pltpu.VMEM((planes + 2 * BLOCK, rows, cols), F32),
             pltpu.VMEM((planes + 2 * BLOCK, rows, cols), F32),
             pltpu.VMEM((bits - 1, 2, planes, rows // 4, cols), F32),
             pltpu.VMEM((bits, 2, planes, rows // 4, cols), F32),
-            pltpu.VMEM((3, planes + BLOCK, rows, cols), F32),
+            pltpu.VMEM(raw_shape, F32),
             pltpu.VMEM((3, BLOCK // GROUP, 3 * grows, cols), BF16),
             pltpu.VMEM((5, (planes + BLOCK) * rows, cols), F32),
-            pltpu.VMEM((3, grows, 3 * cols), BF16),
-            pltpu.VMEM((3, planes, rows, cols), F32),
             pltpu.VMEM((rows, cols), F32),
             pltpu.VMEM((size, 8, 128), F32),
             dma((chunks,)),
-            dma((stages, 2, chunks)),
-            dma((stages, 2, chunks)),
+            dma((stages, 2, pieces)),
+            dma((stages, 2, pieces)),
             dma((2, 2)),
             dma((2, 2)),
             dma((size,)),
             dma((size,)),
-            dma((planes // GROUP + chunks,)),
+            dma((chunks + 2,)),
         ],
         compiler_params=pltpu.CompilerParams(
             collective_id=0, has_side_effects=True, vmem_limit_bytes=60 * 1024 * 1024
         ),
         cost_estimate=pl.CostEstimate(
-            flops=300 * cells, bytes_accessed=20 * cells, transcendentals=0
+            flops=200 * cells, bytes_accessed=20 * cells, transcendentals=0
         ),
-    )(warped, by, bx, gy, gx)
+    )(warped, by, bx)
+    force, template = pl.pallas_call(
+        functools.partial(blur_kernel, weights),
+        out_shape=(
+            jax.ShapeDtypeStruct((1, 3, planes, rows, cols), F32),
+            jax.ShapeDtypeStruct((planes, rows, cols), F32),
+        ),
+        in_specs=[anywhere, anywhere, vmem, vmem],
+        out_specs=(anywhere, anywhere),
+        scratch_shapes=[
+            pltpu.VMEM(raw_shape, F32),
+            pltpu.VMEM((3, grows, 3 * cols), BF16),
+            pltpu.VMEM((3, planes, rows, cols), F32),
+            dma((chunks + 2,)),
+            dma((planes // GROUP,)),
+        ],
+        compiler_params=pltpu.CompilerParams(vmem_limit_bytes=60 * 1024 * 1024),
+        cost_estimate=pl.CostEstimate(
+            flops=100 * cells, bytes_accessed=32 * cells, transcendentals=0
+        ),
+    )(raw, mean, gy, gx)
     return (force, template, loss)
 
 

time: 82.3 us -> 132 us (1.60)
  Pallas kernels: 71.1 us -> 129 us
  local copies, waits for them, and re-layouts: 7.77 us -> 0 us
    pallas_call x1 -> x2, Pallas kernels: 71.1 us -> 129 us  [the longest x1 65.9 us: on_device(): pl.pallas_call(functools.partial(blur_kernel, weights), out_shape=(jax.Sh...]
    unnamed x4 -> x0, local copies, waits for them, and re-layouts: 7.77 us -> none
where the time goes in v3:
time: 132 us
  Pallas kernels  129 us (98%)
  between operations  2.46 us (2%)
    pallas_call x1, Pallas kernels, on_device(): pl.pallas_call(functools.partial(blur_kernel, weights), out_shape=(jax.Sh...  65.9 us
    pallas_call x1, Pallas kernels, on_device(): pl.pallas_call(functools.partial(kernel, (members, size)), out_shape=(jax...  63.2 us

profile of v3, /device:TPU:0, one launch (start us, length us, event | category | flops | bytes accessed | tf_op | source)
XLA Modules:
  0.0 131.5 jit_solution(3962819312718045876)
XLA Ops:
  0.6 63.2 %shard_map.76 = (f32[3,40,64,256]{3,2,1,0:T(8,128)}, f32[32,64,256]{2,1,0:T(8,128)}, f32[1]{0:T(128)}) custom-call(f32[1,32,64,256]{3,2,1,0:T(8,128)} %x.1, bf16[256,768]{1,0:T(8,128)(2,1)} %constant.8.clone.by, bf16[768,256]{1,0:T(8,128)(2,1)} %constant.9.clone.bx), custom_call_target="tpu_custom_call" | custom-call | flops 104857600 | bytes 10485760 | tf_op jit(solution)/shard_map/pallas_call | solution.py:528
  63.9 65.9 %shard_map.77 = (f32[1,3,32,64,256]{4,3,2,1,0:T(8,128)}, f32[32,64,256]{2,1,0:T(8,128)}) custom-call(f32[3,40,64,256]{3,2,1,0:T(8,128)} %get-tuple-element.8.raw, f32[32,64,256]{2,1,0:T(8,128)} %get-tuple-element.9.mean, bf16[256,768]{1,0:T(8,128)(2,1)} %constant.10.clone.gy, bf16[768,256]{1,0:T(8,128)(2,1)} %constant.11.clone.gx), custom_call_target="tpu_custom_call" | custom-call | flops 52428800 | bytes 16777216 | tf_op jit(solution)/shard_map/pallas_call | solution.py:563

commit v4 on v3

--- a/solution.py
+++ b/solution.py
@@ -327,14 +327,12 @@
                 copy.wait_send()
 
     edge = BLOCK // PIECE
-    order = list(range(edge)) + list(range(pieces - edge, pieces))
-    order += list(range(edge, pieces - edge))
-    ahead = 4
+    ahead = 3
 
     def first(pos):
         if pos < pieces:
             for h in range(2):
-                step(0, h, order[pos]).start()
+                step(0, h, pos).start()
 
     for pos in range(ahead):
         first(pos)
@@ -355,35 +353,31 @@
 
     loss[...] = jnp.zeros_like(loss)
     blocks = chunks + 1
-    last = 2 * (stages - 1)
-    events = sorted((pos + 2 * s, -s, pos) for s in range(stages) for pos in range(pieces))
+    last = stages - 1
+    events = sorted((pos + s, -s, pos) for s in range(stages) for pos in range(pieces))
 
     def need(slot):
-        b = 0 if slot == 0 else chunks if slot == 1 else slot - 1
-        cells = [c for c in range((b - 1) * edge, (b + 1) * edge) if 0 <= c < pieces]
-        return last + max(order.index(c) for c in cells)
+        return last + min(pieces, edge * (slot + 2)) - 1
 
     def place(key):
-        if key < last + 2:
-            return 0, key * blocks // (last + 2)
-        if key <= last + 2 * edge - 1:
-            return 1, 0
-        if key == last + 2 * edge:
-            return 2, 0
-        if key == last + 2 * edge + 1:
-            return 1, 1
-        return 1, min(t for t in range(blocks) if need(t) >= key)
+        if key < need(0):
+            return 0, key * blocks // need(0)
+        slot = min(t for t in range(blocks) if need(t) >= key)
+        return (1, slot) if key == need(slot) else (2, slot - 1)
 
     def serve(kind, slot):
         for key, s, pos in events:
             if place(key) == (kind, slot):
-                finish(-s, order[pos])
+                finish(-s, pos)
                 if s == 0:
                     first(pos + ahead)
                 if -s == stages - 1 and pos == edge - 1:
                     halo(1, 0, 0, "start")
-                if -s == stages - 1 and pos == 2 * edge - 1:
+                if -s == stages - 1 and pos == pieces - 1:
                     halo(1, 1, 0, "start")
+
+    def block_of(i):
+        return jnp.where(i < chunks, i + 1, 0)
 
     for load in loads:
         load.wait()
@@ -395,12 +389,11 @@
             def _(slot=slot):
                 serve(0, slot)
                 if slot == chunks - 1:
+                    halo(0, 0, 1, "wait")
+                if slot == chunks:
                     halo(0, 1, 1, "wait")
-                if slot == chunks:
-                    halo(0, 0, 1, "wait")
-
-        b = jnp.where(i < chunks - 1, i + 1, (i - chunks + 1) * chunks)
-        box_block(b, 0, 2, iw, jw, xy, t_ref, by, bx)
+
+        box_block(block_of(i), 0, 2, iw, jw, xy, t_ref, by, bx)
         return 0
 
     lax.fori_loop(0, blocks, moving_part, 0)
@@ -415,17 +408,19 @@
             @pl.when(i == slot)
             def _(slot=slot):
                 serve(1, slot)
-                if slot == 0:
+                if slot == chunks - 1:
+                    halo(1, 0, 1, "wait")
+                if slot == chunks:
                     halo(1, 1, 1, "wait")
-                if slot == 1:
-                    halo(1, 0, 1, "wait")
-
-        b = jnp.where(i == 0, 0, jnp.where(i == 1, chunks, i - 1))
+
+        b = block_of(i)
         box_block(b, 2, 3, iw, jw, xy, t_ref, by, bx)
 
-        @pl.when(i == 0)
-        def _():
-            serve(2, 0)
+        for slot in range(chunks - 1):
+
+            @pl.when(i == slot)
+            def _(slot=slot):
+                serve(2, slot)
 
         force_block(b, z_first, depth, planes, iw, jw, r_ref, t_ref, loss)
         raw_copy(b).start()
@@ -475,7 +470,7 @@
             halo(which, way, 0, "wait")
 
 
-def blur_kernel(weights, raw, mean, gy, gx, out, template, r_ref, yx, out_v, load_sem, put_sem):
+def blur_kernel(weights, raw, mean, gy, gx, out, template, r_ref, yx, out_v, mean_v, load_sem, put_sem):
     planes, rows, cols = out.shape[2:]
     blocks = raw.shape[1] // BLOCK
 
@@ -485,8 +480,9 @@
 
     for b in range(blocks):
         load(b).start()
-    whole = pltpu.make_async_copy(mean, template, load_sem.at[blocks])
-    whole.start()
+    mean_in = pltpu.make_async_copy(mean, mean_v, load_sem.at[blocks])
+    mean_out = pltpu.make_async_copy(mean_v, template, put_sem.at[planes // GROUP])
+    mean_in.start()
     load(0).wait()
 
     def put(k, base, value):
@@ -501,6 +497,11 @@
         def _():
             load(g // (BLOCK // GROUP) + 1).wait()
 
+        @pl.when(g == planes // GROUP - 4)
+        def _():
+            mean_in.wait()
+            mean_out.start()
+
         blur_block(g, weights, r_ref, yx, gy, gx, put)
         put_copy(g).start()
         return 0
@@ -508,7 +509,7 @@
     lax.fori_loop(0, planes // GROUP, blur, 0)
     for g in range(planes // GROUP):
         put_copy(g).wait()
-    whole.wait()
+    mean_out.wait()
 
 
 def on_device(warped):
@@ -572,8 +573,9 @@
             pltpu.VMEM(raw_shape, F32),
             pltpu.VMEM((3, grows, 3 * cols), BF16),
             pltpu.VMEM((3, planes, rows, cols), F32),
+            pltpu.VMEM((planes, rows, cols), F32),
             dma((chunks + 2,)),
-            dma((planes // GROUP,)),
+            dma((planes // GROUP + 1,)),
         ],
         compiler_params=pltpu.CompilerParams(vmem_limit_bytes=60 * 1024 * 1024),
         cost_estimate=pl.CostEstimate(

time: 132 us -> 85.6 us (0.65)
  Pallas kernels: 129 us -> 83 us
    pallas_call x1, Pallas kernels: 65.9 us -> 16.5 us  [on_device(): pl.pallas_call(functools.partial(blur_kernel, weights), out_shape=(jax.Sh...]
    pallas_call x1, Pallas kernels: 63.2 us -> 66.5 us  [on_device(): pl.pallas_call(functools.partial(kernel, (members, size)), out_shape=(jax...]
where the time goes in v4:
time: 85.6 us; the launch traced here: 85.4 us
  Pallas kernels  83 us (97%)
  between operations  2.46 us (3%)
    pallas_call x1, Pallas kernels, on_device(): pl.pallas_call(functools.partial(kernel, (members, size)), out_shape=(jax...  66.5 us
    pallas_call x1, Pallas kernels, on_device(): pl.pallas_call(functools.partial(blur_kernel, weights), out_shape=(jax.Sh...  16.5 us

profile of v4, /device:TPU:0, one launch (start us, length us, event | category | flops | bytes accessed | tf_op | source)
XLA Modules:
  0.0 85.4 jit_solution(2719208293977550099)
XLA Ops:
  0.6 66.5 %shard_map.76 = (f32[3,40,64,256]{3,2,1,0:T(8,128)}, f32[32,64,256]{2,1,0:T(8,128)}, f32[1]{0:T(128)}) custom-call(f32[1,32,64,256]{3,2,1,0:T(8,128)} %x.1, bf16[256,768]{1,0:T(8,128)(2,1)} %constant.8.clone.by, bf16[768,256]{1,0:T(8,128)(2,1)} %constant.9.clone.bx), custom_call_target="tpu_custom_call" | custom-call | flops 104857600 | bytes 10485760 | tf_op jit(solution)/shard_map/pallas_call | solution.py:529
  67.1 16.5 %shard_map.77 = (f32[1,3,32,64,256]{4,3,2,1,0:T(8,128)}, f32[32,64,256]{2,1,0:T(8,128)}) custom-call(f32[3,40,64,256]{3,2,1,0:T(8,128)} %get-tuple-element.8.raw, f32[32,64,256]{2,1,0:T(8,128)} %get-tuple-element.9.mean, bf16[256,768]{1,0:T(8,128)(2,1)} %constant.10.clone.gy, bf16[768,256]{1,0:T(8,128)(2,1)} %constant.11.clone.gx), custom_call_target="tpu_custom_call" | custom-call | flops 52428800 | bytes 16777216 | tf_op jit(solution)/shard_map/pallas_call | solution.py:564

commit v5 on v4

--- a/solution.py
+++ b/solution.py
@@ -16,7 +16,7 @@
 BLOCK = 8
 GROUP = 4
 STRIP = 16
-PIECE = 4
+PIECE = 8
 F32 = jnp.float32
 BF16 = jnp.bfloat16
 MESH = pl.DeviceIdType.MESH
@@ -89,13 +89,14 @@
     grows = GROUP * rows
     span = BLOCK + 2 * BOX_R
 
-    def strip(s, _):
-        row = pl.multiple_of(s * STRIP, STRIP)
-        for lane in range(0, cols, 128):
-            iv = [iw[base + k, pl.ds(row, STRIP), pl.ds(lane, 128)] for k in range(span)]
-            if first + count > 2:
-                jv = [jw[base + k, pl.ds(row, STRIP), pl.ds(lane, 128)] for k in range(span)]
-            for v in range(first, first + count):
+    def strips(v):
+        for row in range(0, rows, STRIP):
+            for lane in range(0, cols, 128):
+                at = (pl.ds(row, STRIP), pl.ds(lane, 128))
+                if v in (0, 1, 4):
+                    iv = [iw[(base + k,) + at] for k in range(span)]
+                if v > 1:
+                    jv = [jw[(base + k,) + at] for k in range(span)]
                 if v == 0:
                     vol = iv
                 elif v == 1:
@@ -109,23 +110,21 @@
                 for w, total in enumerate(windows(vol)):
                     g, u = w // GROUP, w % GROUP
                     for k, piece in enumerate(split3(total)):
-                        at = k * grows + u * rows
-                        xy[v - first, g, pl.ds(at + row, STRIP), pl.ds(lane, 128)] = piece
-        return 0
-
-    lax.fori_loop(0, rows // STRIP, strip, 0)
-
-    def group(g, _):
+                        low = k * grows + u * rows + row
+                        xy[v - first, g, pl.ds(low, STRIP), pl.ds(lane, 128)] = piece
+
+    def products(v, g):
         at = pl.multiple_of(b * BLOCK * rows + g * grows, grows)
-        for v in range(count):
-            ys = jnp.dot(by[...], xy[v, g], preferred_element_type=F32)
-            xs = jnp.concatenate(split3(ys), axis=1)
-            t_ref[first + v, pl.ds(at, grows), :] = jnp.dot(
-                xs, bx[...], preferred_element_type=F32
-            )
-        return 0
-
-    lax.fori_loop(0, BLOCK // GROUP, group, 0)
+        ys = jnp.dot(by[...], xy[v - first, g], preferred_element_type=F32)
+        xs = jnp.concatenate(split3(ys), axis=1)
+        t_ref[v, pl.ds(at, grows), :] = jnp.dot(xs, bx[...], preferred_element_type=F32)
+
+    strips(first)
+    for v in range(first, first + count):
+        if v + 1 < first + count:
+            strips(v + 1)
+        for g in range(BLOCK // GROUP):
+            products(v, g)
 
 
 def force_block(b, z_first, depth, planes, iw, jw, r_ref, t_ref, loss):
@@ -171,10 +170,8 @@
     rows, cols = r_ref.shape[2], r_ref.shape[3]
     base = b * GROUP
 
-    for k in range(3):
-
-        def strip(s, _):
-            row = pl.multiple_of(s * STRIP, STRIP)
+    def strips(k):
+        for row in range(0, rows, STRIP):
             for lane in range(0, cols, 128):
                 v = [
                     r_ref[k, base + BOX_R - GAUSS_R + j, pl.ds(row, STRIP), pl.ds(lane, 128)]
@@ -190,14 +187,18 @@
                     yx[k, pl.ds(at, STRIP), pl.ds(lane, 128)] = high
                     yx[k, pl.ds(at, STRIP), pl.ds(cols + lane, 128)] = low
                     yx[k, pl.ds(at, STRIP), pl.ds(2 * cols + lane, 128)] = high
-            return 0
-
-        lax.fori_loop(0, rows // STRIP, strip, 0)
-    for k in range(3):
+
+    def products(k):
         xs = jnp.dot(yx[k], gx[...], preferred_element_type=F32)
         high, low = split2(xs)
         both = jnp.concatenate([high, low, high], axis=0)
         put(k, base, jnp.dot(gy[...], both, preferred_element_type=F32))
+
+    strips(0)
+    for k in range(3):
+        if k < 2:
+            strips(k + 1)
+        products(k)
 
 
 def kernel(
@@ -327,7 +328,7 @@
                 copy.wait_send()
 
     edge = BLOCK // PIECE
-    ahead = 3
+    ahead = 2
 
     def first(pos):
         if pos < pieces:
@@ -353,21 +354,24 @@
 
     loss[...] = jnp.zeros_like(loss)
     blocks = chunks + 1
-    last = stages - 1
-    events = sorted((pos + s, -s, pos) for s in range(stages) for pos in range(pieces))
+    last = 3 * (stages - 1)
+    events = sorted((2 * pos + 3 * s, -s, pos) for s in range(stages) for pos in range(pieces))
 
     def need(slot):
-        return last + min(pieces, edge * (slot + 2)) - 1
-
-    def place(key):
-        if key < need(0):
-            return 0, key * blocks // need(0)
+        return last + 2 * (min(pieces, edge * (slot + 2)) - 1)
+
+    def place(event):
+        key = event[0]
+        if key <= need(0):
+            index = events.index(event)
+            return (0, index) if index < blocks else (1, 0)
         slot = min(t for t in range(blocks) if need(t) >= key)
         return (1, slot) if key == need(slot) else (2, slot - 1)
 
     def serve(kind, slot):
-        for key, s, pos in events:
-            if place(key) == (kind, slot):
+        for event in events:
+            key, s, pos = event
+            if place(event) == (kind, slot):
                 finish(-s, pos)
                 if s == 0:
                     first(pos + ahead)

time: 85.6 us -> 72.6 us (0.85)
  Pallas kernels: 83 us -> 70 us
    pallas_call x1, Pallas kernels: 66.5 us -> 56.3 us  [on_device(): pl.pallas_call(functools.partial(kernel, (members, size)), out_shape=(jax...]
    pallas_call x1, Pallas kernels: 16.5 us -> 13.7 us  [on_device(): pl.pallas_call(functools.partial(blur_kernel, weights), out_shape=(jax.Sh...]
where the time goes in v5:
time: 72.6 us; the launch traced here: 72.5 us
  Pallas kernels  70 us (96%)
  between operations  2.46 us (3%)
    pallas_call x1, Pallas kernels, on_device(): pl.pallas_call(functools.partial(kernel, (members, size)), out_shape=(jax...  56.3 us
    pallas_call x1, Pallas kernels, on_device(): pl.pallas_call(functools.partial(blur_kernel, weights), out_shape=(jax.Sh...  13.7 us

profile of v5, /device:TPU:0, one launch (start us, length us, event | category | flops | bytes accessed | tf_op | source)
XLA Modules:
  0.0 72.5 jit_solution(892006314132053927)
XLA Ops:
  0.6 56.3 %shard_map.76 = (f32[3,40,64,256]{3,2,1,0:T(8,128)}, f32[32,64,256]{2,1,0:T(8,128)}, f32[1]{0:T(128)}) custom-call(f32[1,32,64,256]{3,2,1,0:T(8,128)} %x.1, bf16[256,768]{1,0:T(8,128)(2,1)} %constant.8.clone.by, bf16[768,256]{1,0:T(8,128)(2,1)} %constant.9.clone.bx), custom_call_target="tpu_custom_call" | custom-call | flops 104857600 | bytes 10485760 | tf_op jit(solution)/shard_map/pallas_call | solution.py:533
  56.9 13.7 %shard_map.77 = (f32[1,3,32,64,256]{4,3,2,1,0:T(8,128)}, f32[32,64,256]{2,1,0:T(8,128)}) custom-call(f32[3,40,64,256]{3,2,1,0:T(8,128)} %get-tuple-element.8.raw, f32[32,64,256]{2,1,0:T(8,128)} %get-tuple-element.9.mean, bf16[256,768]{1,0:T(8,128)(2,1)} %constant.10.clone.gy, bf16[768,256]{1,0:T(8,128)(2,1)} %constant.11.clone.gx), custom_call_target="tpu_custom_call" | custom-call | flops 52428800 | bytes 16777216 | tf_op jit(solution)/shard_map/pallas_call | solution.py:568
